TPU v7x, 256 devices: a whole 4x4x8 slice. The times are simulated.
256 devices in a mesh: dx: 8 (over x, core), dy: 32 (over z, y).
Axes of the slice: x: 4, y: 4, z: 8, core: 2. Of those that a mesh axis runs over, the one named last changes fastest.
Arguments:
- moments: float32 [35, 65536], P(None, ('dx', 'dy')), may hold values from -4 to 4
- positions: float32 [3, 131072, 128], P(None, ('dx', 'dy')), may hold values from -0.5 to 0.5
- masses: float32 [131072, 128], P(('dx', 'dy')), may hold values from 0.004 to 0.04
- counts: int32 [131072], P(('dx', 'dy')), may hold values from 1 to 128
- node_links: int32 [256, 3, 8, 128], P(('dx', 'dy')), may hold values from -1 to 342, as said below
- leaf_links: int32 [256, 3, 8, 128], P(('dx', 'dy')), may hold values from -1 to 511, as said below
- node_local: int32 [256, 3, 2048], P(('dx', 'dy')), may hold values from 0 to 342, as said below
- leaf_local: int32 [256, 3, 128], P(('dx', 'dy')), may hold values from 0 to 511, as said below
Outputs:
- local_exp: float32 [35, 65536], P(None, ('dx', 'dy'))
- forces: float32 [3, 131072, 128], P(None, ('dx', 'dy'))
Inputs may be any that keep to these rules, and one draw needn't show every extreme that they name: `node_links`: slot s of column block a of domain p belongs to peer domain a * 32 + s // 4, never p itself. Field 0 is the domain's own node, or -1 for an empty slot; field 1 is the peer's node; field 2 is a node code whose offset has a largest magnitude of 2 or 3. Peers more than 8 domains away from p along the domain order (taken cyclically over all domains) use at most one slot. Every domain fills all 4 slots of peer p + 1 (cyclically). `leaf_links`: slot s of column block a of domain p belongs to peer domain a * 32 + s // 4, never p itself. Field 0 is the domain's own leaf, or -1 for an empty slot; field 1 is the peer's leaf; field 2 is a leaf code other than 13. Only peers p + 1, p - 1, p + 2, p - 2, p + 32 and p - 32 (cyclically over all domains) have used slots. Every domain fills all 4 slots of peer p + 1. `node_local`: Fields: two different nodes of the domain and a node code whose offset has a largest magnitude of 2 or 3. `leaf_local`: Fields: two different leaves of the domain and a leaf code other than 13.
All inputs are finite; a program needn't handle non-finite values.
Results may differ from a plain program's by a relative error of at most 0.0003.
Values sent between devices are 32-bit elements; how exact they have to be, the bound alone decides.
No kernel may reach another device: no remote copies, remote signals or barrier semaphores. Data moves between devices by JAX's collectives and lax.ppermute only.
A program may use at most 64 MiB of HBM per device.

v0:
```python
import math

import jax
import jax.numpy as jnp
from jax import lax
from jax.sharding import PartitionSpec as P

softening = 0.04


def multi_indices():
    listed = []
    for order in range(5):
        for first in range(order, -1, -1):
            for second in range(order - first, -1, -1):
                listed.append((first, second, order - first - second))
    return listed


def shift_table():
    listed = multi_indices()
    position_of = {entry: number for number, entry in enumerate(listed)}
    rows = []
    for left in listed:
        for right in listed:
            joined = (left[0] + right[0], left[1] + right[1], left[2] + right[2])
            row = [0.0] * len(listed)
            if sum(joined) <= 4:
                row[position_of[joined]] = 1.0
            rows.append(row)
    return jnp.array(rows, dtype=jnp.float32)


def order_signs():
    return jnp.array(
        [1.0 if sum(entry) % 2 == 0 else -1.0 for entry in multi_indices()], dtype=jnp.float32
    )


def derivatives(sep_x, sep_y, sep_z):
    inverse = 1.0 / jnp.sqrt(sep_x * sep_x + sep_y * sep_y + sep_z * sep_z)
    inverse_sq = inverse * inverse
    terms = {}
    power = inverse
    factor = 1.0
    for level in range(5):
        terms[0, 0, 0, level] = factor * power
        power = power * inverse_sq
        factor = factor * -(2 * level + 1)
    for order in range(1, 5):
        for entry in multi_indices():
            if sum(entry) != order:
                continue
            first, second, third = entry
            for level in range(5 - order):
                if first > 0:
                    value = sep_x * terms[first - 1, second, third, level + 1]
                    if first > 1:
                        value = value + (first - 1) * terms[first - 2, second, third, level + 1]
                elif second > 0:
                    value = sep_y * terms[first, second - 1, third, level + 1]
                    if second > 1:
                        value = value + (second - 1) * terms[first, second - 2, third, level + 1]
                else:
                    value = sep_z * terms[first, second, third - 1, level + 1]
                    if third > 1:
                        value = value + (third - 1) * terms[first, second, third - 2, level + 1]
                terms[first, second, third, level] = value
    return jnp.stack([terms[entry[0], entry[1], entry[2], 0] for entry in multi_indices()])


def node_tile(near_moments, far_moments, codes, lives):
    sep_x = (codes // 49 - 3).astype(jnp.float32)
    sep_y = (codes // 7 % 7 - 3).astype(jnp.float32)
    sep_z = (codes % 7 - 3).astype(jnp.float32)
    deriv = derivatives(sep_x, sep_y, sep_z)
    count = len(multi_indices())
    spread = jnp.dot(shift_table(), deriv, precision=lax.Precision.HIGHEST).reshape(
        count, count, -1
    )
    signs = order_signs()[:, None]
    to_far = -jnp.einsum(
        "kjp,jp->kp", spread, signs * near_moments, precision=lax.Precision.HIGHEST
    )
    to_near = -signs * jnp.einsum(
        "kjp,jp->kp", spread, far_moments, precision=lax.Precision.HIGHEST
    )
    return (to_near * lives[None, :], to_far * lives[None, :])


def leaf_tile(near, far, codes, lives):
    shifts = (
        (codes // 9 - 1).astype(jnp.float32),
        (codes // 3 % 3 - 1).astype(jnp.float32),
        (codes % 3 - 1).astype(jnp.float32),
    )
    parts = []
    for axis in range(3):
        moved = far[axis] + shifts[axis][:, None]
        parts.append(moved[:, None, :] - near[axis][:, :, None])
    squared = parts[0] * parts[0] + parts[1] * parts[1] + parts[2] * parts[2] + softening
    inverse = 1.0 / jnp.sqrt(squared)
    weight = inverse * inverse * inverse
    by_far = weight * far[3][:, None, :]
    by_near = weight * near[3][:, :, None]
    pull_near = jnp.stack([jnp.sum(by_far * part, axis=2) for part in parts])
    pull_far = jnp.stack([-jnp.sum(by_near * part, axis=1) for part in parts])
    return (pull_near * lives[None, :, None], pull_far * lives[None, :, None])


def blockwise(tile, inputs, axes, width, passes, outputs):

    def step(number, carried):
        start = number * width
        pieces = [
            lax.dynamic_slice_in_dim(item, start, width, axis) for item, axis in zip(inputs, axes)
        ]
        results = tile(*pieces)
        return tuple(
            (
                lax.dynamic_update_slice_in_dim(held, fresh, start, 1)
                for held, fresh in zip(carried, results)
            )
        )

    empty = tuple((jnp.zeros(shape, jnp.float32) for shape in outputs))
    return lax.fori_loop(0, passes, step, empty)


def node_blocks(near, far, codes, lives):
    total = codes.shape[0]
    width = math.gcd(total, 128)
    coefs = near.shape[0]
    return blockwise(
        node_tile,
        (near, far, codes, lives),
        (1, 1, 0, 0),
        width,
        total // width,
        ((coefs, total), (coefs, total)),
    )


def leaf_blocks(near, far, codes, lives):
    total = codes.shape[0]
    width = math.gcd(total, 32)
    outputs = ((3, total, near.shape[2]), (3, total, near.shape[2]))
    return blockwise(
        leaf_tile, (near, far, codes, lives), (1, 1, 0, 0), width, total // width, outputs
    )


def cross_leaves(near, far, codes, lives):
    pull_near, pull_far = leaf_blocks(near, far, codes, lives)
    return (pull_near, pull_far)


def on_device(moments, positions, masses, counts, node_links, leaf_links, node_local, leaf_local):
    coefs = moments.shape[0]
    cells = masses.shape[1]
    slot_index = lax.broadcasted_iota(jnp.int32, masses.shape, 1)
    live_cells = (slot_index < counts[:, None]).astype(jnp.float32)
    sources = jnp.concatenate([positions, (masses * live_cells)[None]], axis=0)
    node_table = node_links[0]
    leaf_table = leaf_links[0]
    slabs = node_table.shape[1]
    node_slots = node_table.shape[2]
    leaf_slots = leaf_table.shape[2]
    node_keep = jnp.maximum(node_table[0], 0).reshape(-1)
    leaf_keep = jnp.maximum(leaf_table[0], 0).reshape(-1)
    node_alive = (node_table[0] >= 0).astype(jnp.float32).reshape(-1)
    leaf_alive = (leaf_table[0] >= 0).astype(jnp.float32).reshape(-1)
    asked_nodes, asked_leaves = (
        lax.all_to_all(
            lax.all_to_all(node_table[1], "dx", split_axis=0, concat_axis=0, tiled=True),
            "dy",
            split_axis=1,
            concat_axis=1,
            tiled=True,
        ),
        lax.all_to_all(
            lax.all_to_all(leaf_table[1], "dx", split_axis=0, concat_axis=0, tiled=True),
            "dy",
            split_axis=1,
            concat_axis=1,
            tiled=True,
        ),
    )
    first_nodes = node_local[0, 0]
    second_nodes = node_local[0, 1]
    inner_near, inner_far = node_blocks(
        moments[:, first_nodes],
        moments[:, second_nodes],
        node_local[0, 2],
        jnp.ones(first_nodes.shape, jnp.float32),
    )
    local_exp = (
        jnp.zeros(moments.shape, jnp.float32)
        .at[:, first_nodes]
        .add(inner_near)
        .at[:, second_nodes]
        .add(inner_far)
    )
    first_leaves = leaf_local[0, 0]
    second_leaves = leaf_local[0, 1]
    near_pull, far_pull = leaf_blocks(
        sources[:, first_leaves],
        sources[:, second_leaves],
        leaf_local[0, 2],
        jnp.ones(first_leaves.shape, jnp.float32),
    )
    pull = (
        jnp.zeros(positions.shape, jnp.float32)
        .at[:, first_leaves]
        .add(near_pull)
        .at[:, second_leaves]
        .add(far_pull)
    )
    wanted_nodes = asked_nodes.reshape(-1)
    wanted_leaves = asked_leaves.reshape(-1)
    sent_moments = moments[:, wanted_nodes].reshape(coefs, slabs, node_slots)
    sent_cells = sources[:, wanted_leaves].reshape(4, slabs, leaf_slots, cells)
    got_moments, got_cells = (
        lax.all_to_all(
            lax.all_to_all(sent_moments, "dx", split_axis=1, concat_axis=1, tiled=True),
            "dy",
            split_axis=2,
            concat_axis=2,
            tiled=True,
        ),
        lax.all_to_all(
            lax.all_to_all(sent_cells, "dx", split_axis=1, concat_axis=1, tiled=True),
            "dy",
            split_axis=2,
            concat_axis=2,
            tiled=True,
        ),
    )
    to_near, to_far = node_blocks(
        moments[:, node_keep], got_moments.reshape(coefs, -1), node_table[2].reshape(-1), node_alive
    )
    cross_near, cross_far = cross_leaves(
        sources[:, leaf_keep],
        got_cells.reshape(4, -1, cells),
        leaf_table[2].reshape(-1),
        leaf_alive,
    )
    back_local, back_pull = (
        lax.all_to_all(
            lax.all_to_all(
                to_far.reshape(coefs, slabs, node_slots),
                "dx",
                split_axis=1,
                concat_axis=1,
                tiled=True,
            ),
            "dy",
            split_axis=2,
            concat_axis=2,
            tiled=True,
        ),
        lax.all_to_all(
            lax.all_to_all(
                cross_far.reshape(3, slabs, leaf_slots, cells),
                "dx",
                split_axis=1,
                concat_axis=1,
                tiled=True,
            ),
            "dy",
            split_axis=2,
            concat_axis=2,
            tiled=True,
        ),
    )
    local_exp = (
        local_exp.at[:, node_keep]
        .add(to_near)
        .at[:, wanted_nodes]
        .add(back_local.reshape(coefs, -1))
    )
    pull = (
        pull.at[:, leaf_keep]
        .add(cross_near)
        .at[:, wanted_leaves]
        .add(back_pull.reshape(3, -1, cells))
    )
    return (local_exp, pull * live_cells[None])


def solution(mesh):
    in_specs = (
        P(None, ("dx", "dy")),
        P(None, ("dx", "dy"), None),
        P(("dx", "dy"), None),
        P(("dx", "dy")),
        P(("dx", "dy"), None, None, None),
        P(("dx", "dy"), None, None, None),
        P(("dx", "dy"), None, None),
        P(("dx", "dy"), None, None),
    )
    out_specs = (P(None, ("dx", "dy")), P(None, ("dx", "dy"), None))
    return jax.shard_map(
        on_device, mesh=mesh, in_specs=in_specs, out_specs=out_specs, check_vma=False
    )
```

profile of v0, /device:TPU:10, one launch (start us, length us, event | category | flops | bytes accessed | tf_op | source)
XLA Modules:
  0.0 802.0 jit_solution(2723686708640950507)
XLA Ops:
  19.0 11.7 %all-to-all-start.1 = ((s32[8,32,4]{0,2,1:T(4,128)}), s32[8,32,4]{0,2,1:T(4,128)S(1)}, u32[]{:S(2)}, u32[]{:S(2)}) async-start(s32[8,32,4]{0,2,1:T(4,128)} %bitcast.47), calls=%async_computation.1 | async-start | bytes 131072 | tf_op jit(solution)/shard_map/all_to_all | solution.py:174
  69.7 8.0 gather_fusion.6
  83.9 7.9 gather_fusion.7
  92.4 7.6 gather_fusion
  102.4 7.6 gather_fusion.1
  126.5 9.6 %all-to-all-start.9 = ((f32[4,8,128,128]{3,0,1,2:T(4,128)}), f32[4,8,128,128]{3,0,1,2:T(4,128)}, u32[]{:S(2)}, u32[]{:S(2)}) async-start(f32[4,8,128,128]{3,0,1,2:T(4,128)} %copy.185), calls=%async_computation.9 | async-start | bytes 4194304 | tf_op jit(solution)/shard_map/all_to_all | solution.py:231
  136.5 60.6 %while.79 = (s32[]{:T(128)}, f32[35,1024]{1,0:T(8,128)S(1)}, f32[35,1024]{1,0:T(8,128)S(1)}, f32[35,1024]{1,0:T(8,128)S(1)}, s32[1024]{0:T(1024)S(1)}, /*index=5...) while((s32[]{:T(128)}, f32[35,1024]{1,0:T(8,128)S(1)}, ...), condition=%wide.region_5.6_spmd.clone.clone, body=%wide.region_4.5_spmd.sunk.clone.clone.sunk | while | flops 11482758 | bytes 2969675 | solution.py:127
  151.9 6.1 fusion.116
  159.5 6.1 fusion.116
  167.1 6.1 fusion.116
  174.7 6.1 fusion.116
  182.2 6.1 fusion.116
  208.2 272.9 %while.77 = (s32[]{:T(128)}, f32[3,1024,128]{2,1,0:T(8,128)S(1)}, f32[3,1024,128]{2,1,0:T(8,128)}, f32[4,1024,128]{2,1,0:T(8,128)}, s32[1024]{0:T(1024)S(1)}, /*...) while((s32[]{:T(128)}, f32[3,1024,128]{2,1,0:T(8,128)S(1)}, ...), condition=%wide.region_25.26_spmd, body=%wide.region_18.0_spmd.sunk | while | flops 13181897 | bytes 788359 | solution.py:127
  489.4 131.7 %while.78 = (s32[]{:T(128)}, f32[35,2048]{1,0:T(8,128)S(1)}, f32[35,2048]{1,0:T(8,128)S(1)}, f32[35,2048]{1,0:T(8,128)}, s32[2048]{0:T(1024)S(1)}, /*index=5*/f3...) while((s32[]{:T(128)}, f32[35,2048]{1,0:T(8,128)S(1)}, ...), condition=%wide.region_1.2_spmd.clone.clone, body=%wide.region_0.1_spmd.sunk.clone.clone.sunk | while | flops 11473798 | bytes 2968131 | solution.py:127
  622.6 10.1 %all-to-all-start.5 = ((f32[32,1,1120]{2,1,0:T(1,128)}), f32[32,1,1120]{2,1,0:T(1,128)S(1)}, u32[]{:S(2)}, u32[]{:S(2)}) async-start(f32[32,1,1120]{2,1,0:T(1,128)} %reshape.921), calls=%async_computation.5 | async-start | bytes 294912 | tf_op jit(solution)/shard_map/all_to_all | solution.py:249
  641.7 6.5 all-to-all-start.11
  648.2 22.1 %while.76 = (s32[]{:T(128)}, f32[3,128,128]{2,1,0:T(8,128)S(1)}, f32[3,128,128]{2,1,0:T(8,128)S(1)}, f32[4,128,128]{2,0,1:T(4,128)S(1)}, s32[128]{0:T(128)S(1)},...) while((s32[]{:T(128)}, f32[3,128,128]{2,1,0:T(8,128)S(1)}, ...), condition=%wide.region_15.16_spmd, body=%wide.region_8.0_spmd.sunk | while | flops 13157321 | bytes 885879 | solution.py:127
  673.2 8.9 %scatter_fusion.3 = f32[3,512,128]{2,0,1:T(4,128)S(1)} fusion(f32[3,512,128]{2,0,1:T(4,128)S(1)} %broadcast_in_dim.78, s32[128]{0:T(128)S(1)} %get-tuple-element.1404, f32[128,3,128]{2,1,0:T(4,128)} %copy.181), kind=kCustom, calls=%fused_computation.12 | custom fusion | flops 49152 | bytes 590336 | tf_op jit(solution)/shard_map/scatter-add | solution.py:215
  687.0 11.9 %scatter_custom_fusion = f32[35,256]{0,1:T(8,128)S(1)} fusion(s32[2048]{0:T(1024)} %bitcast.296, f32[2048,35]{1,0:T(8,128)} %copy.163, f32[]{:T(128)} %constant.574.clone.1), kind=kCustom, calls=%fused_computation.339 | custom fusion | flops 71680 | bytes 36352 | tf_op jit(solution)/shard_map/scatter-add | solution.py:200
  698.9 11.5 %scatter_fusion = f32[35,256]{0,1:T(8,128)S(1)} fusion(f32[35,256]{0,1:T(8,128)S(1)} %scatter_custom_fusion, s32[2048]{0:T(1024)S(1)} %bitcast.290, f32[2048,35]{1,0:T(8,128)S(1)} %copy.164), kind=kCustom, calls=%fused_computation.9 | custom fusion | flops 71680 | bytes 868352 | tf_op jit(solution)/shard_map/scatter-add | solution.py:202
  710.8 6.4 scatter_fusion.1
  719.4 6.3 scatter_fusion.2
  728.9 36.0 %scatter_fusion.5 = f32[3,512,128]{2,0,1:T(4,128)S(1)} fusion(f32[3,512,128]{2,0,1:T(4,128)S(1)} %scatter_fusion.4, s32[1024]{0:T(1024)S(1)} %copy-done.52, f32[1024,3,128]{2,1,0:T(4,128)S(1)} %copy.188), kind=kCustom, calls=%fused_computation.14 | custom fusion | flops 393216 | bytes 4722688 | tf_op jit(solution)/shard_map/scatter-add | solution.py:284
  767.7 32.8 %scatter_fusion.6 = f32[3,512,128]{2,0,1:T(4,128)S(1)} fusion(f32[3,512,128]{2,0,1:T(4,128)S(1)} %scatter_fusion.5, s32[1024]{0:T(1024)S(1)} %bitcast.294, f32[1024,3,128]{2,1,0:T(4,128)S(1)} %copy.192), kind=kCustom, calls=%fused_computation.15 | custom fusion | flops 393216 | bytes 4722688 | tf_op jit(solution)/shard_map/scatter-add | solution.py:286
  (874 shorter events, 583.7 us)
Async XLA Ops:
  0.6 32.8 %copy-start.42 = (f32[35,256]{1,0:T(8,128)S(1)}, f32[35,256]{1,0:T(8,128)}, u32[]{:S(2)}) copy-start(f32[35,256]{1,0:T(8,128)} %param.20) | copy-start | bytes 107524
  2.0 8.6 %all-to-all-start = ((s32[8,1,128]{2,1,0:T(1,128)}), s32[8,1,128]{2,1,0:T(1,128)S(1)}, u32[]{:S(2)}, u32[]{:S(2)}) async-start(s32[8,1,128]{2,1,0:T(1,128)} %bitcast.46), calls=%async_computation | async-start | bytes 8192 | tf_op jit(solution)/shard_map/all_to_all | solution.py:175
  10.5 8.5 %all-to-all-start.6 = ((s32[8,1,128]{2,1,0:T(1,128)}), s32[8,1,128]{2,1,0:T(1,128)S(1)}, u32[]{:S(2)}, u32[]{:S(2)}) async-start(s32[8,1,128]{2,1,0:T(1,128)} %bitcast.67), calls=%async_computation.6 | async-start | bytes 8192 | tf_op jit(solution)/shard_map/all_to_all | solution.py:182
  19.0 20.4 %all-to-all-start.1 = ((s32[8,32,4]{0,2,1:T(4,128)}), s32[8,32,4]{0,2,1:T(4,128)S(1)}, u32[]{:S(2)}, u32[]{:S(2)}) async-start(s32[8,32,4]{0,2,1:T(4,128)} %bitcast.47), calls=%async_computation.1 | async-start | bytes 131072 | tf_op jit(solution)/shard_map/all_to_all | solution.py:174
  39.4 13.8 %all-to-all-start.7 = ((s32[8,32,4]{0,2,1:T(4,128)}), s32[8,32,4]{0,2,1:T(4,128)S(1)}, u32[]{:S(2)}, u32[]{:S(2)}) async-start(s32[8,32,4]{0,2,1:T(4,128)} %bitcast.68), calls=%async_computation.7 | async-start | bytes 131072 | tf_op jit(solution)/shard_map/all_to_all | solution.py:181
  53.1 9.8 %all-to-all-start.2 = ((f32[35,8,128]{2,0,1:T(8,128)}), f32[35,8,128]{2,0,1:T(8,128)S(1)}, u32[]{:S(2)}, u32[]{:S(2)}) async-start(f32[35,8,128]{2,0,1:T(8,128)} %copy.168), calls=%async_computation.2 | async-start | bytes 327680 | tf_op jit(solution)/shard_map/all_to_all | solution.py:225
  64.4 14.4 %all-to-all-start.3 = ((f32[32,1,1120]{2,1,0:T(1,128)}), f32[32,1,1120]{2,1,0:T(1,128)S(1)}, u32[]{:S(2)}, u32[]{:S(2)}) async-start(f32[32,1,1120]{2,1,0:T(1,128)} %reshape.919), calls=%async_computation.3 | async-start | bytes 294912 | tf_op jit(solution)/shard_map/all_to_all | solution.py:224
  78.8 45.4 %all-to-all-start.8 = ((f32[4,8,128,128]{3,0,2,1:T(4,128)}), f32[4,8,128,128]{3,0,2,1:T(4,128)S(1)}, u32[]{:S(2)}, u32[]{:S(2)}) async-start(f32[4,8,128,128]{3,0,2,1:T(4,128)} %bitcast.71), calls=%async_computation.8 | async-start | bytes 4194304 | tf_op jit(solution)/shard_map/all_to_all | solution.py:232
  91.8 10.5 %copy-start.49 = (s32[2048,1]{0,1:T(1,128)}, s32[2048,1]{0,1:T(1,128)S(1)}, u32[]{:S(2)}) copy-start(s32[2048,1]{0,1:T(1,128)S(1)} %get-tuple-element.1396) | copy-start | bytes 24580
  126.1 10.1 %copy-start.4 = (f32[1225]{0:T(1024)S(1)}, f32[1225]{0:T(1024)}, u32[]{:S(2)}) copy-start(f32[1225]{0:T(1024)} %constant.1138) | copy-start | bytes 14704
  126.1 10.1 %copy-start.5 = (f32[1225]{0:T(1024)S(1)}, f32[1225]{0:T(1024)}, u32[]{:S(2)}) copy-start(f32[1225]{0:T(1024)} %constant.1139) | copy-start | bytes 14704
  126.1 10.1 %copy-start.6 = (f32[1225]{0:T(1024)S(1)}, f32[1225]{0:T(1024)}, u32[]{:S(2)}) copy-start(f32[1225]{0:T(1024)} %constant.1140) | copy-start | bytes 14704
  126.1 10.1 %copy-start.7 = (f32[1225]{0:T(1024)S(1)}, f32[1225]{0:T(1024)}, u32[]{:S(2)}) copy-start(f32[1225]{0:T(1024)} %constant.1141) | copy-start | bytes 14704
  126.1 10.1 %copy-start.8 = (f32[1225]{0:T(1024)S(1)}, f32[1225]{0:T(1024)}, u32[]{:S(2)}) copy-start(f32[1225]{0:T(1024)} %constant.1142) | copy-start | bytes 14704
  126.5 71.4 %all-to-all-start.9 = ((f32[4,8,128,128]{3,0,1,2:T(4,128)}), f32[4,8,128,128]{3,0,1,2:T(4,128)}, u32[]{:S(2)}, u32[]{:S(2)}) async-start(f32[4,8,128,128]{3,0,1,2:T(4,128)} %copy.185), calls=%async_computation.9 | async-start | bytes 4194304 | tf_op jit(solution)/shard_map/all_to_all | solution.py:231
  197.9 286.6 %all-to-all-start.4 = ((f32[35,8,128]{2,0,1:T(8,128)}), f32[35,8,128]{2,0,1:T(8,128)S(1)}, u32[]{:S(2)}, u32[]{:S(2)}) async-start(f32[35,8,128]{2,0,1:T(8,128)} %copy.174), calls=%async_computation.4 | async-start | bytes 327680 | tf_op jit(solution)/shard_map/all_to_all | solution.py:250
  484.5 138.1 %all-to-all-start.10 = ((f32[3,8,128,128]{3,2,0,1:T(8,128)}), f32[3,8,128,128]{3,2,0,1:T(8,128)}, u32[]{:S(2)}, u32[]{:S(2)}) async-start(f32[3,8,128,128]{3,2,0,1:T(8,128)} %copy.189), calls=%async_computation.10 | async-start | bytes 3145728 | tf_op jit(solution)/shard_map/all_to_all | solution.py:263
  489.4 131.7 %copy-start.54 = (s32[1,3,128]{2,0,1:T(1,128)S(1)}, s32[1,3,128]{2,0,1:T(1,128)}, u32[]{:S(2)}) copy-start(s32[1,3,128]{2,0,1:T(1,128)} %param.27) | copy-start | bytes 4612
  622.6 19.1 %all-to-all-start.5 = ((f32[32,1,1120]{2,1,0:T(1,128)}), f32[32,1,1120]{2,1,0:T(1,128)S(1)}, u32[]{:S(2)}, u32[]{:S(2)}) async-start(f32[32,1,1120]{2,1,0:T(1,128)} %reshape.921), calls=%async_computation.5 | async-start | bytes 294912 | tf_op jit(solution)/shard_map/all_to_all | solution.py:249
  641.7 123.2 %all-to-all-start.11 = ((f32[3,8,128,128]{3,1,0,2:T(8,128)}), f32[3,8,128,128]{3,1,0,2:T(8,128)}, u32[]{:S(2)}, u32[]{:S(2)}) async-start(f32[3,8,128,128]{3,1,0,2:T(8,128)} %copy.190), calls=%async_computation.11 | async-start | bytes 3145728 | tf_op jit(solution)/shard_map/all_to_all | solution.py:262
  672.7 26.2 %copy-start.39 = (s32[2048,1]{0,1:T(1,128)S(1)}, s32[2048,1]{0,1:T(1,128)}, u32[]{:S(2)}) copy-start(s32[2048,1]{0,1:T(1,128)} %copy-done.38) | copy-start | bytes 24580
  698.9 11.6 %copy-start.53 = (s32[512]{0:T(512)S(1)}, s32[512]{0:T(512)}, u32[]{:S(2)}) copy-start(s32[512]{0:T(512)} %param.23) | copy-start | bytes 6148
  698.9 11.7 %copy-start.37 = (f32[35,1024]{1,0:T(8,128)S(1)}, f32[35,1024]{1,0:T(8,128)}, u32[]{:S(2)}) copy-start(f32[35,1024]{1,0:T(8,128)} %copy-done.36) | copy-start | bytes 430084
  698.9 11.9 %copy-start.51 = (s32[1024]{0:T(1024)S(1)}, s32[1024]{0:T(1024)}, u32[]{:S(2)}) copy-start(s32[1024]{0:T(1024)} %get-tuple-element.1401) | copy-start | bytes 12292
  (44 other events, 386.1 us)
where the time goes:
time: 818 us; the launch traced here: 802 us
  other arithmetic  536 us (66%)
  local copies, waits for them, and re-layouts  160 us (20%)
  starting transfers between devices  77 us (9%)
  waiting for transfers between devices  23.8 us (3%)
    reduce_sum x36, other arithmetic, leaf_tile(): pull_far = jnp.stack([-jnp.sum(by_near * part, axis=1) for part in parts])  179 us
    dot_general x24, other arithmetic, node_tile(): jnp.dot(shift_table(), deriv, precision=lax.Precision.HIGHEST)  147 us
    scatter-add x2, other arithmetic, on_device(): pull = pull.at[:, leaf_keep].add(cross_near).at[:, wanted_leaves].add(bac...  68.8 us
    slice x36, local copies, waits for them, and re-layouts, leaf_tile(): parts.append(moved[:, None, :] - near[axis][:, :, None])  35 us
    add x44, other arithmetic, leaf_tile(): moved = far[axis] + shifts[axis][:, None]  27.7 us
    dynamic_update_slice x60, other arithmetic, step(): lax.dynamic_update_slice_in_dim(held, fresh, start, 1)  24.2 us
    scatter-add x2, other arithmetic, on_device(): local_exp = jnp.zeros(moments.shape, jnp.float32).at[:, first_nodes].add(...  23.4 us
    mul x32, local copies, waits for them, and re-layouts, leaf_tile(): by_far = weight * far[3][:, None, :]  23.3 us
  transfers between devices with their start and end apart: 12, of which 7 were waited for; matrix products, arithmetic and copies ran while one was open for 82% of the time, Pallas kernels for 0%

commit v1 on v0

v1 whole, which is shorter than its diff:
```python
import functools

import jax
import jax.numpy as jnp
from jax import lax
from jax.experimental import pallas as pl
from jax.experimental.pallas import tpu as pltpu
from jax.sharding import PartitionSpec as P

softening = 0.04
DOMAINS = 256
SUBS = 32
SHIFTS = (32, -32, -2, -1, 2, 1)
F32, BF16, I32 = jnp.float32, jnp.bfloat16, jnp.int32
PEER_NODE, NODE_CODE, PEER_LEAF, LEAF_CODE, OWN_NODE = 25, 26, 27, 28, 29


def multi_indices():
    listed = []
    for order in range(5):
        for first in range(order, -1, -1):
            for second in range(order - first, -1, -1):
                listed.append((first, second, order - first - second))
    return listed


ALL = multi_indices()
KEPT = [entry for entry in ALL if entry[2] <= 1]
RANK = len(KEPT)


def reduce_rows(moments):
    rows = {entry: moments[number : number + 1, :] for number, entry in enumerate(ALL)}
    for entry in sorted(ALL, key=lambda item: -item[2]):
        first, second, third = entry
        if third > 1:
            for other in ((first + 2, second, third - 2), (first, second + 2, third - 2)):
                rows[other] = rows[other] - rows[entry]
    blank = jnp.zeros((32 - RANK, moments.shape[1]), F32)
    return jnp.concatenate([rows[entry] for entry in KEPT] + [blank], axis=0)


def expand_rows(total, out_ref):
    rows = {entry: total[number : number + 1, :] for number, entry in enumerate(KEPT)}
    for entry in sorted(ALL, key=lambda item: item[2]):
        first, second, third = entry
        if third > 1:
            rows[entry] = -(rows[first + 2, second, third - 2] + rows[first, second + 2, third - 2])
    for number, entry in enumerate(ALL):
        out_ref[number : number + 1, :] = rows[entry]


def split(value, terms):
    pieces = []
    for _ in range(terms - 1):
        high = value.astype(BF16)
        pieces.append(high)
        value = value - high.astype(F32)
    pieces.append(value.astype(BF16))
    return pieces


def one_hot(row, count):
    numbers = lax.broadcasted_iota(I32, (count, row.shape[1]), 0)
    return jnp.where(numbers == row, 1.0, 0.0).astype(BF16)


def pick(table3, hot):
    got = jnp.dot(table3, hot, preferred_element_type=F32)
    return got[0:32] + got[32:64] + got[64:96]


def put(values, hot):
    got = lax.dot_general(
        jnp.concatenate(split(values, 2), axis=0),
        hot,
        (((1,), (1,)), ((), ())),
        preferred_element_type=F32,
    )
    return got[0:32] + got[32:64]


def derivative_terms(codes):
    sep_x = ((codes * 1338) >> 16).astype(I32)
    rest = codes - sep_x * 49
    sep_y = (rest * 37) >> 8
    sep_z = rest - sep_y * 7
    sep = [(part - 3).astype(F32) for part in (sep_x, sep_y, sep_z)]
    squared = sep[0] * sep[0] + sep[1] * sep[1] + sep[2] * sep[2]
    inverse = lax.rsqrt(squared)
    inverse = inverse * (1.5 - 0.5 * squared * (inverse * inverse))
    inverse_sq = inverse * inverse
    known = {}
    power, factor = inverse, 1.0
    for level in range(5):
        known[0, 0, 0, level] = factor * power
        power = power * inverse_sq
        factor = factor * -(2 * level + 1)

    def term(first, second, third, level):
        key = (first, second, third, level)
        if key not in known:
            entry = [first, second, third]
            axis = 0 if first else (1 if second else 2)
            entry[axis] -= 1
            value = sep[axis] * term(*entry, level + 1)
            if entry[axis] > 0:
                scale = entry[axis]
                entry[axis] -= 1
                lower = term(*entry, level + 1)
                value = value + (lower if scale == 1 else scale * lower)
            known[key] = value
        return known[key]

    return {entry: term(*entry, 0) for entry in ALL if entry[2] <= 2}


def node_sums(codes, load_near, load_far, store_near, store_far):
    deriv = derivative_terms(codes)
    near = [load_near(number) for number in range(RANK)]
    far = [load_far(number) for number in range(RANK)]
    for k, left in enumerate(KEPT):
        even = {True: None, False: None}
        to_near = None
        for j, right in enumerate(KEPT):
            if sum(left) + sum(right) > 4:
                continue
            d = deriv[left[0] + right[0], left[1] + right[1], left[2] + right[2]]
            side = sum(right) % 2 == 0
            product = d * near[j]
            even[side] = product if even[side] is None else even[side] + product
            product = d * far[j]
            to_near = product if to_near is None else to_near + product
        to_far = -even[True] if even[False] is None else even[False] - even[True]
        store_far(k, to_far)
        store_near(k, to_near if sum(left) % 2 else -to_near)


def strided(ref, base, number):
    return ref[pl.ds(base + number, 8, stride=32), :]


def peer_of(shift):
    me = lax.axis_index("dx") * SUBS + lax.axis_index("dy")
    return (me + shift + DOMAINS) % DOMAINS


def pack_kernel(moments_hbm, nodes_hbm, leaves_hbm, kept_ref, sent_ref, moments_ref, nodes_ref, leaves_ref, sems):
    copies = [
        pltpu.make_async_copy(source, target, sems.at[number])
        for number, (source, target) in enumerate(
            ((nodes_hbm, nodes_ref), (leaves_hbm, leaves_ref), (moments_hbm, moments_ref))
        )
    ]
    for copy in copies:
        copy.start()
    for copy in copies:
        copy.wait()
    kept = reduce_rows(moments_ref[...])
    kept_ref[...] = kept
    table3 = jnp.concatenate(split(kept, 3), axis=0)
    own, peer_node, node_code = (nodes_ref[0, field] for field in range(3))
    leaf, peer_leaf, leaf_code = (leaves_ref[0, field] for field in range(3))
    fields = [
        own,
        jnp.where(own >= 0, peer_node, 0),
        jnp.where(own >= 0, node_code, 0),
        jnp.where(leaf >= 0, peer_leaf, -1),
        jnp.where(leaf >= 0, leaf_code, 0),
    ]
    stacked = jnp.concatenate([field.astype(F32) for field in fields], axis=0)
    source = lax.broadcasted_iota(I32, (128, 128), 0)
    target = lax.broadcasted_iota(I32, (128, 128), 1)
    lanes = jnp.where((source & 3) * 32 + (source >> 2) == target, 1.0, 0.0).astype(BF16)
    got = jnp.dot(jnp.concatenate(split(stacked, 2), axis=0), lanes, preferred_element_type=F32)
    moved = got[0:40] + got[40:80]
    block = lax.broadcasted_iota(I32, (128, 128), 0) >> 5 == (
        lax.broadcasted_iota(I32, (128, 128), 1) >> 5
    )
    row_number = lax.broadcasted_iota(I32, (8, 128), 0)
    for slab in range(8):
        rows = [moved[8 * field + slab : 8 * field + slab + 1] for field in range(5)]
        values = pick(table3, one_hot(rows[0].astype(I32), 256))
        last = values[24:32]
        for field, lane in ((0, OWN_NODE), (1, PEER_NODE), (2, NODE_CODE), (3, PEER_LEAF), (4, LEAF_CODE)):
            last = jnp.where(row_number == lane - 24, rows[field], last)
        values = jnp.concatenate([values[0:24], last], axis=0)
        turned = jnp.where(block, jnp.concatenate([values] * 4, axis=0), 0.0).T
        sent_ref[32 * slab : 32 * slab + 32, :] = (
            turned[0:32] + turned[32:64] + turned[64:96] + turned[96:128]
        )


def answer_kernel(
    links_ref, counts_ref, got_ref, kept_ref, positions_ref, masses_ref,
    reply_ref, partial_ref, asked_ref, cells_ref,
    turned, far_side, near_out, far_out, whole, rows, sems,
):
    whole[...] = got_ref[...].astype(I32)
    copies = []
    peers = [peer_of(shift) for shift in SHIFTS] + [peer_of(-shift) for shift in SHIFTS]
    for number in range(12):
        first = pl.multiple_of((peers[number] >> 3) * 8, 8)
        copies.append(
            pltpu.make_async_copy(whole.at[pl.ds(first, 8)], rows.at[number], sems.at[number])
        )
        copies[-1].start()
    for half in range(2):
        turned[128 * half : 128 * half + 128, :] = got_ref[128 * half : 128 * half + 128, :].T
    table3 = jnp.concatenate(split(kept_ref[...], 3), axis=0)
    for group in range(8):
        row = turned[32 * group + PEER_NODE : 32 * group + PEER_NODE + 1, :].astype(I32)
        far_side[32 * group : 32 * group + 32, :] = pick(table3, one_hot(row, 256))

    def store_near(number, value):
        near_out[pl.ds(number, 8, stride=32), :] = value

    def store_far(number, value):
        far_out[pl.ds(number, 8, stride=32), :] = value

    for number in range(RANK, 32):
        store_near(number, jnp.zeros((8, 128), F32))
        store_far(number, jnp.zeros((8, 128), F32))
    node_sums(
        strided(turned, 0, NODE_CODE).astype(I32),
        functools.partial(strided, turned, 0),
        functools.partial(strided, far_side, 0),
        store_near,
        store_far,
    )
    for half in range(2):
        reply_ref[128 * half : 128 * half + 128, :] = near_out[128 * half : 128 * half + 128, :].T
    total = jnp.zeros((32, 256), F32)
    for group in range(8):
        row = turned[32 * group + PEER_NODE : 32 * group + PEER_NODE + 1, :].astype(I32)
        total = total + put(far_out[32 * group : 32 * group + 32, :], one_hot(row, 256))
    partial_ref[...] = total
    for copy in copies:
        copy.wait()
    lane = lax.broadcasted_iota(I32, (1, 128), 1)

    def fill(number, slot, leaf):
        live = jnp.where(leaf >= 0, counts_ref[jnp.maximum(leaf, 0)], 0)
        leaf = jnp.maximum(leaf, 0)
        for axis in range(3):
            cells_ref[number, 4 * slot + axis : 4 * slot + axis + 1, :] = positions_ref[axis, pl.ds(leaf, 1), :]
        cells_ref[number, 4 * slot + 3 : 4 * slot + 4, :] = jnp.where(
            lane < live, masses_ref[pl.ds(leaf, 1), :], 0.0
        )

    for number in range(12):
        peer = peers[number]
        for slot in range(4):
            asked = rows[number, peer & 7, 32 * slot + PEER_LEAF]
            if number < 6:
                fill(number, slot, links_ref[0, 0, peer >> 5, (peer & 31) * 4 + slot])
                fill(number, 4 + slot, asked)
            else:
                asked_ref[number - 6, 2 * slot] = asked
                asked_ref[number - 6, 2 * slot + 1] = rows[number, peer & 7, 32 * slot + LEAF_CODE]


def leaf_offset(code):
    first = (code * 57) >> 9
    second = (code * 171) >> 9
    third = code - second * 3
    second = second - first * 3
    return [(part - 1).astype(F32) for part in (first, second, third)]


def eight_pairs(fields, left, right, terms_a, terms_b, sums_a, sums_b, pulls_a, pulls_b):
    a, b = ([fields[8 * (base + axis) : 8 * (base + axis) + 8, :] for axis in range(3)] for base in (0, 4))
    mass_a, mass_b = fields[24:32, :], fields[56:64, :]
    one = jnp.ones((8, 128), F32)
    rows_a, rows_b = [], []
    for axis in range(3):
        a1, a2, a3 = [part.astype(F32) for part in split(a[axis], 3)]
        b1, b2, b3 = [part.astype(F32) for part in split(-2.0 * b[axis], 3)]
        rows_a += [a1, a1, a2, a2, a1, a3]
        rows_b += [b1, b2, b1, b2, b3, b1]
    rows_a += [part.astype(F32) for part in split(a[0] * a[0] + a[1] * a[1] + a[2] * a[2] + softening, 3)]
    rows_b += [one] * 3
    rows_a += [one] * 3
    rows_b += [part.astype(F32) for part in split(b[0] * b[0] + b[1] * b[1] + b[2] * b[2], 3)]
    for number in range(24):
        left[pl.ds(number, 8, stride=32), :] = rows_a[number]
        right[pl.ds(number, 8, stride=32), :] = rows_b[number]
    sides = [(a, mass_a, terms_a)] + ([(b, mass_b, terms_b)] if terms_b is not None else [])
    for place, mass, terms in sides:
        for number, value in enumerate([mass * place[0], mass * place[1], mass * place[2], mass]):
            high, low = split(value, 2)
            terms[pl.ds(number, 8, stride=8), :] = high.astype(F32)
            terms[pl.ds(number + 4, 8, stride=8), :] = low.astype(F32)
    blank = jnp.zeros((32, 128), BF16)
    for group in range(2):
        turned = left[128 * group : 128 * group + 128, :].T.astype(BF16)
        block = right[128 * group : 128 * group + 128, :].astype(BF16)
        for half in range(2):
            columns = []
            for pair in (2 * half, 2 * half + 1):
                parts = [blank] * 4
                parts[pair] = block[32 * pair : 32 * pair + 32, :]
                columns.append(jnp.concatenate(parts, axis=0))
            squared = jnp.dot(turned, jnp.concatenate(columns, axis=1), preferred_element_type=F32)
            inverse = lax.rsqrt(squared)
            weight = inverse * (inverse * inverse)
            high, low = split(weight, 2)
            base = 8 * (4 * group + 2 * half)
            use = terms_a[base : base + 16, :].astype(BF16)
            got = jnp.dot(
                jnp.concatenate([use, use], axis=1),
                jnp.concatenate([high, low], axis=0),
                preferred_element_type=F32,
            )
            sums_b[base : base + 8, :] = got[0:8, 0:128]
            sums_b[base + 8 : base + 16, :] = got[8:16, 128:256]
            if terms_b is not None:
                use = terms_b[base : base + 16, :].astype(BF16)
                both = jnp.concatenate(
                    [
                        jnp.concatenate([high[:, 0:128], low[:, 0:128]], axis=1),
                        jnp.concatenate([high[:, 128:256], low[:, 128:256]], axis=1),
                    ],
                    axis=0,
                )
                got = lax.dot_general(
                    jnp.concatenate([use, use], axis=1),
                    both,
                    (((1,), (1,)), ((), ())),
                    preferred_element_type=F32,
                )
                sums_a[base : base + 8, :] = got[0:8, 0:128]
                sums_a[base + 8 : base + 16, :] = got[8:16, 128:256]
    results = [(b, sums_b, pulls_b)] + ([(a, sums_a, pulls_a)] if terms_b is not None else [])
    for own, sums, pulls in results:
        moved = [
            sums[pl.ds(number, 8, stride=8), :] + sums[pl.ds(number + 4, 8, stride=8), :] for number in range(4)
        ]
        for axis in range(3):
            pulls[8 * axis : 8 * axis + 8, :] = moved[axis] - own[axis] * moved[3]


def clear_rows(*refs):
    for ref in refs:
        for number in range(24, 32):
            ref[pl.ds(number, 8, stride=32), :] = jnp.zeros((8, 128), F32)


def local_nodes_kernel(pairs_ref, kept_ref, partial_ref, near_side, far_side, near_out, far_out):
    table3 = jnp.concatenate(split(kept_ref[...], 3), axis=0)
    for number in range(RANK, 32):
        near_out[pl.ds(number, 8, stride=32), :] = jnp.zeros((8, 128), F32)
        far_out[pl.ds(number, 8, stride=32), :] = jnp.zeros((8, 128), F32)
    total = jnp.zeros((32, 256), F32)
    for batch in range(2):
        code_rows = []
        for group in range(8):
            lanes = slice(1024 * batch + 128 * group, 1024 * batch + 128 * group + 128)
            first, second = (one_hot(pairs_ref[0, field : field + 1, lanes], 256) for field in range(2))
            near_side[32 * group : 32 * group + 32, :] = pick(table3, first)
            far_side[32 * group : 32 * group + 32, :] = pick(table3, second)
            code_rows.append(pairs_ref[0, 2:3, lanes])

        def store_near(number, value):
            near_out[pl.ds(number, 8, stride=32), :] = value

        def store_far(number, value):
            far_out[pl.ds(number, 8, stride=32), :] = value

        node_sums(
            jnp.concatenate(code_rows, axis=0),
            functools.partial(strided, near_side, 0),
            functools.partial(strided, far_side, 0),
            store_near,
            store_far,
        )
        for group in range(8):
            lanes = slice(1024 * batch + 128 * group, 1024 * batch + 128 * group + 128)
            first, second = (one_hot(pairs_ref[0, field : field + 1, lanes], 256) for field in range(2))
            total = total + put(near_out[32 * group : 32 * group + 32, :], first)
            total = total + put(far_out[32 * group : 32 * group + 32, :], second)
    partial_ref[...] = total


CHAINS = 4


def local_leaves_kernel(counts_ref, leaf_pairs_ref, positions_ref, masses_ref, pull_ref, *scratch):
    pull_ref[...] = jnp.zeros_like(pull_ref)
    sets = [scratch[9 * chain : 9 * chain + 9] for chain in range(CHAINS)]
    for work in sets:
        clear_rows(work[1], work[2])
    lane = lax.broadcasted_iota(I32, (1, 128), 1)

    def step(number, _):
        ends = []
        for chain, work in enumerate(sets):
            fields = work[0]
            for pair in range(8):
                place = (number * CHAINS + chain) * 8 + pair
                leaf = [leaf_pairs_ref[0, field, place] for field in range(2)]
                offset = leaf_offset(leaf_pairs_ref[0, 2, place])
                live = [counts_ref[leaf[side]] for side in range(2)]
                ends.append((leaf, live))
                for side, sign in ((0, -0.5), (1, 0.5)):
                    for axis in range(3):
                        row = 8 * (4 * side + axis) + pair
                        fields[row : row + 1, :] = positions_ref[axis, pl.ds(leaf[side], 1), :] + sign * offset[axis]
                    row = 8 * (4 * side + 3) + pair
                    fields[row : row + 1, :] = jnp.where(lane < live[side], masses_ref[pl.ds(leaf[side], 1), :], 0.0)
        for work in sets:
            eight_pairs(*work)
        for chain, work in enumerate(sets):
            for pair in range(8):
                leaf, live = ends[8 * chain + pair]
                for side, pulls in ((0, work[7]), (1, work[8])):
                    for axis in range(3):
                        pull_ref[axis, pl.ds(leaf[side], 1), :] += jnp.where(
                            lane < live[side], pulls[8 * axis + pair : 8 * axis + pair + 1, :], 0.0
                        )
        return 0

    lax.fori_loop(0, 16 // CHAINS, step, 0)


def final_kernel(
    links_ref, asked_ref, counts_ref, sent_ref, reply_ref, cross_ref, local_ref,
    cells0, cells1, cells2, cells3, cells4, cells5, positions_ref, pull_ref,
    out_ref, forces_ref,
    turned, turned_reply, fields, left, right, terms_a, sums_b, pulls_b,
):
    for half in range(2):
        part = slice(128 * half, 128 * half + 128)
        turned[part, :] = sent_ref[part, :].T
        turned_reply[part, :] = reply_ref[part, :].T
    total = cross_ref[...] + local_ref[...]
    for group in range(8):
        row = turned[32 * group + OWN_NODE : 32 * group + OWN_NODE + 1, :].astype(I32)
        total = total + put(turned_reply[32 * group : 32 * group + 32, :], one_hot(row, 256))
    expand_rows(total, out_ref)
    forces_ref[...] = pull_ref[...]
    clear_rows(left, right)
    lane = lax.broadcasted_iota(I32, (1, 128), 1)
    for number, cells in enumerate((cells0, cells1, cells2, cells3, cells4, cells5)):
        peer = peer_of(-SHIFTS[number])
        owns, lives = [], []
        for pair in range(8):
            slot = pair % 4
            if pair < 4:
                place = (peer >> 5, (peer & 31) * 4 + slot)
                own, code = links_ref[0, 0, place[0], place[1]], links_ref[0, 2, place[0], place[1]]
                source, sign = 4 + slot, 0.5
            else:
                own, code = asked_ref[number, 2 * slot], asked_ref[number, 2 * slot + 1]
                source, sign = slot, -0.5
            alive = own >= 0
            own = jnp.maximum(own, 0)
            offset = leaf_offset(jnp.where(alive, code, 0))
            owns.append(own)
            lives.append(jnp.where(alive, counts_ref[own], 0))
            for axis in range(3):
                row = 8 * axis + pair
                fields[row : row + 1, :] = (
                    cells[4 * source + axis : 4 * source + axis + 1, :] + sign * offset[axis]
                )
                fields[32 + row : 33 + row, :] = positions_ref[axis, pl.ds(own, 1), :] - sign * offset[axis]
            fields[24 + pair : 25 + pair, :] = cells[4 * source + 3 : 4 * source + 4, :]
        eight_pairs(fields, left, right, terms_a, None, None, sums_b, None, pulls_b)
        for pair in range(8):
            live = lane < lives[pair]
            for axis in range(3):
                forces_ref[axis, pl.ds(owns[pair], 1), :] += jnp.where(
                    live, pulls_b[8 * axis + pair : 8 * axis + pair + 1, :], 0.0
                )


SMEM = pl.BlockSpec(memory_space=pltpu.SMEM)
VMEM = pl.BlockSpec(memory_space=pltpu.VMEM)
HBM = pl.BlockSpec(memory_space=pltpu.HBM)
PARAMS = pltpu.CompilerParams(vmem_limit_bytes=32 * 1024 * 1024)


def exchange(sent):
    return lax.all_to_all(
        sent.reshape(DOMAINS, 1, 128), ("dx", "dy"), split_axis=0, concat_axis=0, tiled=True
    ).reshape(DOMAINS, 128)


def on_device(moments, positions, masses, counts, node_links, leaf_links, node_local, leaf_local):
    shape = jax.ShapeDtypeStruct
    block = pltpu.VMEM((256, 128), F32)
    tiles, pulls = pltpu.VMEM((64, 128), F32), pltpu.VMEM((24, 128), F32)
    kept, sent = pl.pallas_call(
        pack_kernel,
        out_shape=(shape((32, 256), F32), shape((256, 128), F32)),
        in_specs=[HBM] * 3,
        out_specs=(VMEM, VMEM),
        scratch_shapes=[
            pltpu.VMEM(moments.shape, F32),
            pltpu.VMEM(node_links.shape, I32),
            pltpu.VMEM(leaf_links.shape, I32),
            pltpu.SemaphoreType.DMA((3,)),
        ],
        compiler_params=PARAMS,
        name="pack",
    )(moments, node_links, leaf_links)
    got = exchange(sent)
    local_exp = pl.pallas_call(
        local_nodes_kernel,
        out_shape=shape((32, 256), F32),
        in_specs=[VMEM] * 2,
        out_specs=VMEM,
        scratch_shapes=[block] * 4,
        compiler_params=PARAMS,
        cost_estimate=pl.CostEstimate(flops=300_000_000, bytes_accessed=300_000, transcendentals=2048),
        name="local_nodes",
    )(node_local, kept)
    pull = pl.pallas_call(
        local_leaves_kernel,
        out_shape=shape(positions.shape, F32),
        in_specs=[SMEM, SMEM, VMEM, VMEM],
        out_specs=VMEM,
        scratch_shapes=[tiles, block, block, tiles, tiles, tiles, tiles, pulls, pulls] * CHAINS,
        compiler_params=PARAMS,
        cost_estimate=pl.CostEstimate(flops=80_000_000, bytes_accessed=3_000_000, transcendentals=2_100_000),
        name="local_leaves",
    )(counts, leaf_local, positions, masses)
    got, local_exp, pull = lax.optimization_barrier((got, local_exp, pull))
    reply, cross, asked, cells = pl.pallas_call(
        answer_kernel,
        out_shape=(
            shape((256, 128), F32),
            shape((32, 256), F32),
            shape((6, 8), I32),
            shape((6, 32, 128), F32),
        ),
        in_specs=[SMEM, SMEM] + [VMEM] * 4,
        out_specs=(VMEM, VMEM, SMEM, VMEM),
        scratch_shapes=[block] * 4
        + [pltpu.VMEM((256, 128), I32), pltpu.SMEM((12, 8, 128), I32), pltpu.SemaphoreType.DMA((12,))],
        compiler_params=PARAMS,
        name="answer",
    )(leaf_links, counts, got, kept, positions, masses)
    back = exchange(reply)
    moved = [
        lax.ppermute(
            cells[number],
            ("dx", "dy"),
            [(device, (device + shift) % DOMAINS) for device in range(DOMAINS)],
        )
        for number, shift in enumerate(SHIFTS)
    ]
    return pl.pallas_call(
        final_kernel,
        out_shape=(shape(moments.shape, F32), shape(positions.shape, F32)),
        in_specs=[SMEM] * 3 + [VMEM] * 12,
        out_specs=(VMEM, VMEM),
        scratch_shapes=[block, block, tiles, block, block, tiles, tiles, pulls],
        compiler_params=PARAMS,
        name="final",
    )(leaf_links, asked, counts, sent, back, cross, local_exp, *moved, positions, pull)


def solution(mesh):
    in_specs = (
        P(None, ("dx", "dy")),
        P(None, ("dx", "dy"), None),
        P(("dx", "dy"), None),
        P(("dx", "dy")),
        P(("dx", "dy"), None, None, None),
        P(("dx", "dy"), None, None, None),
        P(("dx", "dy"), None, None),
        P(("dx", "dy"), None, None),
    )
    out_specs = (P(None, ("dx", "dy")), P(None, ("dx", "dy"), None))
    return jax.shard_map(
        on_device, mesh=mesh, in_specs=in_specs, out_specs=out_specs, check_vma=False
    )
```

time: 818 us -> 73.4 us (0.09)
  the two profiles are of different devices: /device:TPU:10 before, /device:TPU:7 now
where the time goes in v1:
time: 73.4 us; the launch traced here: 72.5 us
  starting transfers between devices  41.5 us (57%)
  Pallas kernels  24.7 us (34%)
  local copies, waits for them, and re-layouts  4.02 us (5%)
  waiting for transfers between devices  1.45 us (2%)
  between operations  0.8 us (1%)
    all_to_all x2, starting transfers between devices, exchange(): lax.all_to_all(sent.reshape(DOMAINS, 1, 128), ('dx', 'dy'), split_axis=0,...  28.7 us
    ppermute x6, starting transfers between devices, on_device(): lax.ppermute(cells[number], ('dx', 'dy'), [(device, (device + shift) % DO...  12.8 us
    pallas_call x1, Pallas kernels, on_device(): pl.pallas_call(local_leaves_kernel, out_shape=shape(positions.shape, F32)...  12.7 us
    pallas_call x1, Pallas kernels, on_device(): pl.pallas_call(final_kernel, out_shape=(shape(moments.shape, F32), shape(...  4.5 us
    unnamed x22, local copies, waits for them, and re-layouts  4.01 us
    pallas_call x1, Pallas kernels, on_device(): pl.pallas_call(answer_kernel, out_shape=(shape((256, 128), F32), shape((3...  3.83 us
    pallas_call x1, Pallas kernels, on_device(): pl.pallas_call(local_nodes_kernel, out_shape=shape((32, 256), F32), in_sp...  2.41 us
  transfers between devices with their start and end apart: 8, of which 1 were waited for; matrix products, arithmetic and copies ran while one was open for 0% of the time, Pallas kernels for 21%

profile of v1, /device:TPU:7, one launch (start us, length us, event | category | flops | bytes accessed | tf_op | source)
XLA Modules:
  0.0 72.5 jit_solution(1617572885463332782)
XLA Ops:
  0.6 0.0 copy-start.3
  0.6 0.7 copy-done.3
  1.3 0.8 %copy-done.5 = f32[35,256]{1,0:T(8,128)S(1)} copy-done((f32[35,256]{1,0:T(8,128)S(1)}, f32[35,256]{1,0:T(8,128)}, u32[]{:S(2)}) %copy-start.5) | copy-done | bytes 35864
  2.1 0.7 copy-done.6
  2.8 1.3 %pack.1 = (f32[32,256]{1,0:T(8,128)S(1)}, f32[256,128]{1,0:T(8,128)}) custom-call(f32[35,256]{1,0:T(8,128)S(1)} %copy-done.5, s32[1,3,8,128]{3,2,1,0:T(8,128)S(1)} %copy-done.6, s32[1,3,8,128]{3,2,1,0:T(8,128)S(1)} %copy-done.3), custom_call_target="tpu_custom_call" | custom-call | tf_op jit(solution)/shard_map/pack/pallas_call | solution.py:493
  4.1 0.0 copy-start.9
  4.2 0.0 copy-start.8
  4.2 15.0 %all-to-all-start = ((f32[256,1,128]{2,1,0:T(1,128)}), f32[256,1,128]{2,1,0:T(1,128)S(1)}, u32[]{:S(2)}, u32[]{:S(2)}) async-start(f32[256,1,128]{2,1,0:T(1,128)} %bitcast.1), calls=%async_computation | async-start | bytes 262144 | tf_op jit(solution)/shard_map/all_to_all | solution.py:484
  19.2 0.0 copy-start.7
  19.2 0.6 copy-done.7
  19.9 1.1 %copy-done = f32[3,512,128]{2,1,0:T(8,128)S(1)} copy-done((f32[3,512,128]{2,1,0:T(8,128)S(1)}, f32[3,512,128]{2,1,0:T(8,128)}, u32[]{:S(2)}) %copy-start) | copy-done | bytes 786456
  21.0 12.7 %local_leaves.1.pull_ref = f32[3,512,128]{2,1,0:T(8,128)S(1)} custom-call(s32[512]{0:T(512)S(1)} %copy-done.7, s32[1,3,128]{2,1,0:T(4,128)S(1)} %copy.14.leaf_pairs_ref, f32[3,512,128]{2,1,0:T(8,128)S(1)} %copy-done, f32[512,128]{1,0:T(8,128)S(1)} %copy-done.2), custom_call_target="tpu_custom_call" | custom-call | flops 80000000 | bytes 3000000 | tf_op jit(solution)/shard_map/local_leaves/pallas_call | solution.py:518
  33.7 0.0 copy-start.4
  33.7 2.4 %local_nodes.1.local_ref = f32[32,256]{1,0:T(8,128)S(1)} custom-call(s32[1,3,2048]{2,1,0:T(4,128)S(1)} %copy.13.pairs_ref, f32[32,256]{1,0:T(8,128)S(1)} %get-tuple-element.12.kept_ref), custom_call_target="tpu_custom_call" | custom-call | flops 300000000 | bytes 300000 | tf_op jit(solution)/shard_map/local_nodes/pallas_call | solution.py:508
  36.1 0.0 all-to-all-done
  36.2 3.8 %answer.1 = (f32[256,128]{1,0:T(8,128)}, f32[32,256]{1,0:T(8,128)S(1)}, s32[6,8]{1,0:T(8,128)S(1)}, f32[6,32,128]{2,1,0:T(8,128)S(1)}) custom-call(s32[1,3,8,128]{3,2,1,0:T(8,128)S(1)} %copy-done.4, s32[512]{0:T(512)S(1)} %copy-done.7, f32[256,128]{1,0:T(8,128)S(1)} %bitcast.21, f32[32,256]{1,0:T(8,128)S(1)} %get-tuple-element.12.kept_ref, ...), custom_call_target="tpu_custom_call" | custom-call | tf_op jit(solution)/shard_map/answer/pallas_call | solution.py:529
  40.0 13.7 %all-to-all-start.1 = ((f32[256,1,128]{2,1,0:T(1,128)}), f32[256,1,128]{2,1,0:T(1,128)S(1)}, u32[]{:S(2)}, u32[]{:S(2)}) async-start(f32[256,1,128]{2,1,0:T(1,128)} %bitcast.4), calls=%async_computation.1 | async-start | bytes 262144 | tf_op jit(solution)/shard_map/all_to_all | solution.py:484
  53.8 1.3 %collective-permute-start.5 = (f32[32,128]{1,0:T(8,128)S(1)}, f32[32,128]{1,0:T(8,128)S(1)}, u32[]{:S(2)}, u32[]{:S(2)}) collective-permute-start(f32[32,128]{1,0:T(8,128)S(1)} %get-tuple-element.20), channel_id=1, source_target_pairs={{0,1},{1,2},{2,3},{3,4},{4,5},{5,6},{6,7},{7,8},{8,9},{9,10},{10,1... | collective-permute-start | bytes 49160 | tf_op jit(solution)/shard_map/ppermute | solution.py:546
  55.0 2.5 %collective-permute-start.4 = (f32[32,128]{1,0:T(8,128)S(1)}, f32[32,128]{1,0:T(8,128)S(1)}, u32[]{:S(2)}, u32[]{:S(2)}) collective-permute-start(f32[32,128]{1,0:T(8,128)S(1)} %get-tuple-element.21), channel_id=1, source_target_pairs={{0,2},{1,3},{2,4},{3,5},{4,6},{5,7},{6,8},{7,9},{8,10},{9,11},{10,... | collective-permute-start | bytes 49160 | tf_op jit(solution)/shard_map/ppermute | solution.py:546
  57.5 3.5 %collective-permute-start.3 = (f32[32,128]{1,0:T(8,128)S(1)}, f32[32,128]{1,0:T(8,128)S(1)}, u32[]{:S(2)}, u32[]{:S(2)}) collective-permute-start(f32[32,128]{1,0:T(8,128)S(1)} %get-tuple-element.22), channel_id=1, source_target_pairs={{0,255},{1,0},{2,1},{3,2},{4,3},{5,4},{6,5},{7,6},{8,7},{9,8},{10,... | collective-permute-start | bytes 49160 | tf_op jit(solution)/shard_map/ppermute | solution.py:546
  61.0 2.6 %collective-permute-start.2 = (f32[32,128]{1,0:T(8,128)S(1)}, f32[32,128]{1,0:T(8,128)S(1)}, u32[]{:S(2)}, u32[]{:S(2)}) collective-permute-start(f32[32,128]{1,0:T(8,128)S(1)} %get-tuple-element.23), channel_id=1, source_target_pairs={{0,254},{1,255},{2,0},{3,1},{4,2},{5,3},{6,4},{7,5},{8,6},{9,7},{1... | collective-permute-start | bytes 49160 | tf_op jit(solution)/shard_map/ppermute | solution.py:546
  63.6 3.0 %collective-permute-start = (f32[32,128]{1,0:T(8,128)S(1)}, f32[32,128]{1,0:T(8,128)S(1)}, u32[]{:S(2)}, u32[]{:S(2)}) collective-permute-start(f32[32,128]{1,0:T(8,128)S(1)} %get-tuple-element.25), channel_id=1, source_target_pairs={{0,32},{1,33},{2,34},{3,35},{4,36},{5,37},{6,38},{7,39},{8,40},{9,... | collective-permute-start | bytes 49160 | tf_op jit(solution)/shard_map/ppermute | solution.py:546
  66.6 1.4 %collective-permute-done.1.cells1 = f32[32,128]{1,0:T(8,128)S(1)} collective-permute-done((f32[32,128]{1,0:T(8,128)S(1)}, f32[32,128]{1,0:T(8,128)S(1)}, u32[]{:S(2)}, u32[]{:S(2)}) %collective-permute-start.1) | collective-permute-done | bytes 16416 | tf_op jit(solution)/shard_map/ppermute | solution.py:546
  68.0 4.5 %final.1 = (f32[35,256]{1,0:T(8,128)}, f32[3,512,128]{2,1,0:T(8,128)}) custom-call(s32[1,3,8,128]{3,2,1,0:T(8,128)S(1)} %copy-done.4, s32[6,8]{1,0:T(8,128)S(1)} %get-tuple-element.14.asked_ref, s32[512]{0:T(512)S(1)} %copy-done.7, f32[256,128]{1,0:T(8,128)} %get-tuple-element.11.sent_ref, f32[256,128]{1,0:T(8,128)S(1)} %bitcast.20, ...), custom_call_target="tpu_custom_call" | custom-call | tf_op jit(solution)/shard_map/final/pallas_call | solution.py:553
  (20 shorter events, 0.1 us)
Async XLA Ops:
  0.6 0.7 copy-start.3
  1.3 0.8 %copy-start.5 = (f32[35,256]{1,0:T(8,128)S(1)}, f32[35,256]{1,0:T(8,128)}, u32[]{:S(2)}) copy-start(f32[35,256]{1,0:T(8,128)} %moments_hbm.1) | copy-start | bytes 107524
  2.1 0.7 copy-start.6
  2.8 16.4 %copy-start.2 = (f32[512,128]{1,0:T(8,128)S(1)}, f32[512,128]{1,0:T(8,128)}, u32[]{:S(2)}) copy-start(f32[512,128]{1,0:T(8,128)} %masses_ref.3) | copy-start | bytes 786436
  4.1 15.0 %copy-start.9 = (s32[1,3,128]{2,0,1:T(1,128)S(1)}, s32[1,3,128]{2,0,1:T(1,128)}, u32[]{:S(2)}) copy-start(s32[1,3,128]{2,0,1:T(1,128)} %param.15) | copy-start | bytes 4612
  4.2 15.0 %copy-start.8 = (s32[1,3,2048]{2,0,1:T(1,128)S(1)}, s32[1,3,2048]{2,0,1:T(1,128)}, u32[]{:S(2)}) copy-start(s32[1,3,2048]{2,0,1:T(1,128)} %param.14) | copy-start | bytes 73732
  4.2 32.0 %all-to-all-start = ((f32[256,1,128]{2,1,0:T(1,128)}), f32[256,1,128]{2,1,0:T(1,128)S(1)}, u32[]{:S(2)}, u32[]{:S(2)}) async-start(f32[256,1,128]{2,1,0:T(1,128)} %bitcast.1), calls=%async_computation | async-start | bytes 262144 | tf_op jit(solution)/shard_map/all_to_all | solution.py:484
  19.2 0.7 copy-start.7
  19.8 1.1 %copy-start = (f32[3,512,128]{2,1,0:T(8,128)S(1)}, f32[3,512,128]{2,1,0:T(8,128)}, u32[]{:S(2)}) copy-start(f32[3,512,128]{2,1,0:T(8,128)} %positions_ref.5) | copy-start | bytes 2359300
  33.7 2.5 %copy-start.1 = (f32[3,512,128]{2,1,0:T(8,128)S(1)}, f32[3,512,128]{2,1,0:T(8,128)}, u32[]{:S(2)}) copy-start(f32[3,512,128]{2,1,0:T(8,128)} %positions_ref.5) | copy-start | bytes 2359300
  33.7 2.5 %copy-start.4 = (s32[1,3,8,128]{3,2,1,0:T(8,128)S(1)}, s32[1,3,8,128]{3,2,1,0:T(8,128)}, u32[]{:S(2)}) copy-start(s32[1,3,8,128]{3,2,1,0:T(8,128)} %links_ref.3) | copy-start | bytes 36868
  40.0 28.0 %all-to-all-start.1 = ((f32[256,1,128]{2,1,0:T(1,128)}), f32[256,1,128]{2,1,0:T(1,128)S(1)}, u32[]{:S(2)}, u32[]{:S(2)}) async-start(f32[256,1,128]{2,1,0:T(1,128)} %bitcast.4), calls=%async_computation.1 | async-start | bytes 262144 | tf_op jit(solution)/shard_map/all_to_all | solution.py:484
  53.8 9.8 %collective-permute-start.5 = (f32[32,128]{1,0:T(8,128)S(1)}, f32[32,128]{1,0:T(8,128)S(1)}, u32[]{:S(2)}, u32[]{:S(2)}) collective-permute-start(f32[32,128]{1,0:T(8,128)S(1)} %get-tuple-element.20), channel_id=1, source_target_pairs={{0,1},{1,2},{2,3},{3,4},{4,5},{5,6},{6,7},{7,8},{8,9},{9,10},{10,1... | collective-permute-start | bytes 49160 | tf_op jit(solution)/shard_map/ppermute | solution.py:546
  55.0 11.5 %collective-permute-start.4 = (f32[32,128]{1,0:T(8,128)S(1)}, f32[32,128]{1,0:T(8,128)S(1)}, u32[]{:S(2)}, u32[]{:S(2)}) collective-permute-start(f32[32,128]{1,0:T(8,128)S(1)} %get-tuple-element.21), channel_id=1, source_target_pairs={{0,2},{1,3},{2,4},{3,5},{4,6},{5,7},{6,8},{7,9},{8,10},{9,11},{10,... | collective-permute-start | bytes 49160 | tf_op jit(solution)/shard_map/ppermute | solution.py:546
  57.5 9.1 %collective-permute-start.3 = (f32[32,128]{1,0:T(8,128)S(1)}, f32[32,128]{1,0:T(8,128)S(1)}, u32[]{:S(2)}, u32[]{:S(2)}) collective-permute-start(f32[32,128]{1,0:T(8,128)S(1)} %get-tuple-element.22), channel_id=1, source_target_pairs={{0,255},{1,0},{2,1},{3,2},{4,3},{5,4},{6,5},{7,6},{8,7},{9,8},{10,... | collective-permute-start | bytes 49160 | tf_op jit(solution)/shard_map/ppermute | solution.py:546
  61.0 5.6 %collective-permute-start.2 = (f32[32,128]{1,0:T(8,128)S(1)}, f32[32,128]{1,0:T(8,128)S(1)}, u32[]{:S(2)}, u32[]{:S(2)}) collective-permute-start(f32[32,128]{1,0:T(8,128)S(1)} %get-tuple-element.23), channel_id=1, source_target_pairs={{0,254},{1,255},{2,0},{3,1},{4,2},{5,3},{6,4},{7,5},{8,6},{9,7},{1... | collective-permute-start | bytes 49160 | tf_op jit(solution)/shard_map/ppermute | solution.py:546
  63.6 4.4 %collective-permute-start.1 = (f32[32,128]{1,0:T(8,128)S(1)}, f32[32,128]{1,0:T(8,128)S(1)}, u32[]{:S(2)}, u32[]{:S(2)}) collective-permute-start(f32[32,128]{1,0:T(8,128)S(1)} %get-tuple-element.24), channel_id=1, source_target_pairs={{0,224},{1,225},{2,226},{3,227},{4,228},{5,229},{6,230},{7,231},{8... | collective-permute-start | bytes 49160 | tf_op jit(solution)/shard_map/ppermute | solution.py:546
  63.6 4.4 %collective-permute-start = (f32[32,128]{1,0:T(8,128)S(1)}, f32[32,128]{1,0:T(8,128)S(1)}, u32[]{:S(2)}, u32[]{:S(2)}) collective-permute-start(f32[32,128]{1,0:T(8,128)S(1)} %get-tuple-element.25), channel_id=1, source_target_pairs={{0,32},{1,33},{2,34},{3,35},{4,36},{5,37},{6,38},{7,39},{8,40},{9,... | collective-permute-start | bytes 49160 | tf_op jit(solution)/shard_map/ppermute | solution.py:546

commit v2 on v1

--- a/solution.py
+++ b/solution.py
@@ -383,6 +383,38 @@
 
 
 CHAINS = 4
+EARLY = 3
+
+
+def gather_pairs(sets, first_place, counts_ref, leaf_pairs_ref, positions_ref, masses_ref):
+    lane = lax.broadcasted_iota(I32, (1, 128), 1)
+    for chain, work in enumerate(sets):
+        fields = work[0]
+        for pair in range(8):
+            place = first_place + chain * 8 + pair
+            leaf = [leaf_pairs_ref[0, field, place] for field in range(2)]
+            offset = leaf_offset(leaf_pairs_ref[0, 2, place])
+            for side, sign in ((0, -0.5), (1, 0.5)):
+                live = counts_ref[leaf[side]]
+                for axis in range(3):
+                    row = 8 * (4 * side + axis) + pair
+                    fields[row : row + 1, :] = positions_ref[axis, pl.ds(leaf[side], 1), :] + sign * offset[axis]
+                row = 8 * (4 * side + 3) + pair
+                fields[row : row + 1, :] = jnp.where(lane < live, masses_ref[pl.ds(leaf[side], 1), :], 0.0)
+
+
+def scatter_pairs(pulls_of, first_place, counts_ref, leaf_pairs_ref, pull_ref):
+    lane = lax.broadcasted_iota(I32, (1, 128), 1)
+    for chain in range(CHAINS):
+        for pair in range(8):
+            place = first_place + chain * 8 + pair
+            for side in range(2):
+                leaf = leaf_pairs_ref[0, side, place]
+                live = lane < counts_ref[leaf]
+                for axis in range(3):
+                    pull_ref[axis, pl.ds(leaf, 1), :] += jnp.where(
+                        live, pulls_of(chain, side, 8 * axis + pair), 0.0
+                    )
 
 
 def local_leaves_kernel(counts_ref, leaf_pairs_ref, positions_ref, masses_ref, pull_ref, *scratch):
@@ -390,42 +422,35 @@
     sets = [scratch[9 * chain : 9 * chain + 9] for chain in range(CHAINS)]
     for work in sets:
         clear_rows(work[1], work[2])
-    lane = lax.broadcasted_iota(I32, (1, 128), 1)
 
     def step(number, _):
-        ends = []
-        for chain, work in enumerate(sets):
-            fields = work[0]
-            for pair in range(8):
-                place = (number * CHAINS + chain) * 8 + pair
-                leaf = [leaf_pairs_ref[0, field, place] for field in range(2)]
-                offset = leaf_offset(leaf_pairs_ref[0, 2, place])
-                live = [counts_ref[leaf[side]] for side in range(2)]
-                ends.append((leaf, live))
-                for side, sign in ((0, -0.5), (1, 0.5)):
-                    for axis in range(3):
-                        row = 8 * (4 * side + axis) + pair
-                        fields[row : row + 1, :] = positions_ref[axis, pl.ds(leaf[side], 1), :] + sign * offset[axis]
-                    row = 8 * (4 * side + 3) + pair
-                    fields[row : row + 1, :] = jnp.where(lane < live[side], masses_ref[pl.ds(leaf[side], 1), :], 0.0)
+        place = number * (8 * CHAINS)
+        gather_pairs(sets, place, counts_ref, leaf_pairs_ref, positions_ref, masses_ref)
         for work in sets:
             eight_pairs(*work)
-        for chain, work in enumerate(sets):
-            for pair in range(8):
-                leaf, live = ends[8 * chain + pair]
-                for side, pulls in ((0, work[7]), (1, work[8])):
-                    for axis in range(3):
-                        pull_ref[axis, pl.ds(leaf[side], 1), :] += jnp.where(
-                            lane < live[side], pulls[8 * axis + pair : 8 * axis + pair + 1, :], 0.0
-                        )
+        scatter_pairs(
+            lambda chain, side, row: sets[chain][7 + side][row : row + 1, :],
+            place, counts_ref, leaf_pairs_ref, pull_ref,
+        )
         return 0
 
-    lax.fori_loop(0, 16 // CHAINS, step, 0)
+    lax.fori_loop(0, EARLY, step, 0)
+
+
+def late_leaves_kernel(counts_ref, leaf_pairs_ref, positions_ref, masses_ref, late_ref, *scratch):
+    sets = [scratch[9 * chain : 9 * chain + 9] for chain in range(CHAINS)]
+    for work in sets:
+        clear_rows(work[1], work[2])
+    gather_pairs(sets, EARLY * 8 * CHAINS, counts_ref, leaf_pairs_ref, positions_ref, masses_ref)
+    for chain, work in enumerate(sets):
+        eight_pairs(*work)
+        for side in range(2):
+            late_ref[chain, side] = work[7 + side][...]
 
 
 def final_kernel(
     links_ref, asked_ref, counts_ref, sent_ref, reply_ref, cross_ref, local_ref,
-    cells0, cells1, cells2, cells3, cells4, cells5, positions_ref, pull_ref,
+    cells0, cells1, cells2, cells3, cells4, cells5, positions_ref, pull_ref, late_ref, leaf_pairs_ref,
     out_ref, forces_ref,
     turned, turned_reply, fields, left, right, terms_a, sums_b, pulls_b,
 ):
@@ -439,6 +464,10 @@
         total = total + put(turned_reply[32 * group : 32 * group + 32, :], one_hot(row, 256))
     expand_rows(total, out_ref)
     forces_ref[...] = pull_ref[...]
+    scatter_pairs(
+        lambda chain, side, row: late_ref[chain, side, row : row + 1, :],
+        EARLY * 8 * CHAINS, counts_ref, leaf_pairs_ref, forces_ref,
+    )
     clear_rows(left, right)
     lane = lax.broadcasted_iota(I32, (1, 128), 1)
     for number, cells in enumerate((cells0, cells1, cells2, cells3, cells4, cells5)):
@@ -501,20 +530,10 @@
             pltpu.VMEM(leaf_links.shape, I32),
             pltpu.SemaphoreType.DMA((3,)),
         ],
-        compiler_params=PARAMS,
+        compiler_params=pltpu.CompilerParams(vmem_limit_bytes=56 * 1024 * 1024),
         name="pack",
     )(moments, node_links, leaf_links)
     got = exchange(sent)
-    local_exp = pl.pallas_call(
-        local_nodes_kernel,
-        out_shape=shape((32, 256), F32),
-        in_specs=[VMEM] * 2,
-        out_specs=VMEM,
-        scratch_shapes=[block] * 4,
-        compiler_params=PARAMS,
-        cost_estimate=pl.CostEstimate(flops=300_000_000, bytes_accessed=300_000, transcendentals=2048),
-        name="local_nodes",
-    )(node_local, kept)
     pull = pl.pallas_call(
         local_leaves_kernel,
         out_shape=shape(positions.shape, F32),
@@ -525,7 +544,7 @@
         cost_estimate=pl.CostEstimate(flops=80_000_000, bytes_accessed=3_000_000, transcendentals=2_100_000),
         name="local_leaves",
     )(counts, leaf_local, positions, masses)
-    got, local_exp, pull = lax.optimization_barrier((got, local_exp, pull))
+    got, pull = lax.optimization_barrier((got, pull))
     reply, cross, asked, cells = pl.pallas_call(
         answer_kernel,
         out_shape=(
@@ -550,15 +569,36 @@
         )
         for number, shift in enumerate(SHIFTS)
     ]
+    kept_late, leaf_pairs_late, moved[5] = lax.optimization_barrier((kept, leaf_local, moved[5]))
+    local_exp = pl.pallas_call(
+        local_nodes_kernel,
+        out_shape=shape((32, 256), F32),
+        in_specs=[VMEM] * 2,
+        out_specs=VMEM,
+        scratch_shapes=[block] * 4,
+        compiler_params=PARAMS,
+        cost_estimate=pl.CostEstimate(flops=300_000_000, bytes_accessed=300_000, transcendentals=2048),
+        name="local_nodes",
+    )(node_local, kept_late)
+    late = pl.pallas_call(
+        late_leaves_kernel,
+        out_shape=shape((CHAINS, 2, 24, 128), F32),
+        in_specs=[SMEM, SMEM, VMEM, VMEM],
+        out_specs=VMEM,
+        scratch_shapes=[tiles, block, block, tiles, tiles, tiles, tiles, pulls, pulls] * CHAINS,
+        compiler_params=PARAMS,
+        cost_estimate=pl.CostEstimate(flops=20_000_000, bytes_accessed=1_500_000, transcendentals=500_000),
+        name="late_leaves",
+    )(counts, leaf_pairs_late, positions, masses)
     return pl.pallas_call(
         final_kernel,
         out_shape=(shape(moments.shape, F32), shape(positions.shape, F32)),
-        in_specs=[SMEM] * 3 + [VMEM] * 12,
+        in_specs=[SMEM] * 3 + [VMEM] * 13 + [SMEM],
         out_specs=(VMEM, VMEM),
         scratch_shapes=[block, block, tiles, block, block, tiles, tiles, pulls],
         compiler_params=PARAMS,
         name="final",
-    )(leaf_links, asked, counts, sent, back, cross, local_exp, *moved, positions, pull)
+    )(leaf_links, asked, counts, sent, back, cross, local_exp, *moved, positions, pull, late, leaf_local)
 
 
 def solution(mesh):

time: 73.4 us -> 71.2 us (0.970)
  local copies, waits for them, and re-layouts: 4.02 us -> 1.85 us
  Pallas kernels: 24.7 us -> 26.1 us
  waiting for transfers between devices: 1.45 us -> 0.05 us
    pallas_call x0 -> x1, Pallas kernels: none -> 3.55 us  [on_device(): pl.pallas_call(late_leaves_kernel, out_shape=shape((CHAINS, 2, 24, 128),...]
    pallas_call x1, Pallas kernels: 12.7 us -> 9.67 us  [on_device(): pl.pallas_call(local_leaves_kernel, out_shape=shape(positions.shape, F32)...]
    unnamed x22 -> x20, local copies, waits for them, and re-layouts: 4.01 us -> 1.84 us
    ppermute x6, waiting for transfers between devices: 1.41 us -> 0.04 us  [on_device(): lax.ppermute(cells[number], ('dx', 'dy'), [(device, (device + shift) % DO...]
    pallas_call x1, Pallas kernels: 1.31 us -> 2.1 us  [on_device(): pl.pallas_call(pack_kernel, out_shape=(shape((32, 256), F32), shape((256,...]
  transfers between devices with their start and end apart: 8 -> 8, of which waited for: 1 -> 0; matrix products, arithmetic and copies ran while one was open for 0% -> 0% of each run, Pallas kernels for 21% -> 22%
where the time goes in v2:
time: 71.2 us; the launch traced here: 70.9 us
  starting transfers between devices  42.1 us (59%)
  Pallas kernels  26.1 us (37%)
  local copies, waits for them, and re-layouts  1.85 us (3%)
  between operations  0.85 us (1%)
    all_to_all x2, starting transfers between devices, exchange(): lax.all_to_all(sent.reshape(DOMAINS, 1, 128), ('dx', 'dy'), split_axis=0,...  28.7 us
    ppermute x6, starting transfers between devices, on_device(): lax.ppermute(cells[number], ('dx', 'dy'), [(device, (device + shift) % DO...  13.4 us
    pallas_call x1, Pallas kernels, on_device(): pl.pallas_call(local_leaves_kernel, out_shape=shape(positions.shape, F32)...  9.67 us
    pallas_call x1, Pallas kernels, on_device(): pl.pallas_call(final_kernel, out_shape=(shape(moments.shape, F32), shape(...  4.53 us
    pallas_call x1, Pallas kernels, on_device(): pl.pallas_call(answer_kernel, out_shape=(shape((256, 128), F32), shape((3...  3.82 us
    pallas_call x1, Pallas kernels, on_device(): pl.pallas_call(late_leaves_kernel, out_shape=shape((CHAINS, 2, 24, 128),...  3.55 us
    pallas_call x1, Pallas kernels, on_device(): pl.pallas_call(local_nodes_kernel, out_shape=shape((32, 256), F32), in_sp...  2.41 us
    pallas_call x1, Pallas kernels, on_device(): pl.pallas_call(pack_kernel, out_shape=(shape((32, 256), F32), shape((256,...  2.1 us
  transfers between devices with their start and end apart: 8, of which 0 were waited for; matrix products, arithmetic and copies ran while one was open for 0% of the time, Pallas kernels for 22%

profile of v2, /device:TPU:7, one launch (start us, length us, event | category | flops | bytes accessed | tf_op | source)
XLA Modules:
  0.0 70.9 jit_solution(615301985289002645)
XLA Ops:
  0.6 2.1 %pack.1 = (f32[32,256]{1,0:T(8,128)}, f32[256,128]{1,0:T(8,128)}) custom-call(f32[35,256]{1,0:T(8,128)} %moments_hbm.1, s32[1,3,8,128]{3,2,1,0:T(8,128)} %nodes_hbm.1, s32[1,3,8,128]{3,2,1,0:T(8,128)} %links_ref.3), custom_call_target="tpu_custom_call" | custom-call | tf_op jit(solution)/shard_map/pack/pallas_call | solution.py:522
  2.8 0.0 copy-start.8
  2.8 15.0 %all-to-all-start = ((f32[256,1,128]{2,1,0:T(1,128)}), f32[256,1,128]{2,1,0:T(1,128)S(1)}, u32[]{:S(2)}, u32[]{:S(2)}) async-start(f32[256,1,128]{2,1,0:T(1,128)} %bitcast.20), calls=%async_computation | async-start | bytes 262144 | tf_op jit(solution)/shard_map/all_to_all | solution.py:513
  17.7 0.0 copy-start.6
  17.8 0.7 copy-done.6
  18.4 1.1 %copy-done = f32[3,512,128]{2,1,0:T(8,128)S(1)} copy-done((f32[3,512,128]{2,1,0:T(8,128)S(1)}, f32[3,512,128]{2,1,0:T(8,128)}, u32[]{:S(2)}) %copy-start) | copy-done | bytes 786456
  19.6 9.7 %local_leaves.1.pull_ref = f32[3,512,128]{2,1,0:T(8,128)S(1)} custom-call(s32[512]{0:T(512)S(1)} %copy-done.6, s32[1,3,128]{2,1,0:T(4,128)S(1)} %copy.15.leaf_pairs_ref, f32[3,512,128]{2,1,0:T(8,128)S(1)} %copy-done, f32[512,128]{1,0:T(8,128)S(1)} %copy-done.2), custom_call_target="tpu_custom_call" | custom-call | flops 80000000 | bytes 3000000 | tf_op jit(solution)/shard_map/local_leaves/pallas_call | solution.py:537
  29.2 0.0 all-to-all-done
  29.3 3.8 %answer.1 = (f32[256,128]{1,0:T(8,128)}, f32[32,256]{1,0:T(8,128)S(1)}, s32[6,8]{1,0:T(8,128)S(1)}, f32[6,32,128]{2,1,0:T(8,128)S(1)}) custom-call(s32[1,3,8,128]{3,2,1,0:T(8,128)S(1)} %copy-done.4, s32[512]{0:T(512)S(1)} %copy-done.6, f32[256,128]{1,0:T(8,128)S(1)} %bitcast.22, f32[32,256]{1,0:T(8,128)S(1)} %copy-done.5, f32[3,512,128]{2,1,0:T(8,128)S(1)} %copy-done.1, ...), custom_call_target="tpu_custom_call" | custom-call | tf_op jit(solution)/shard_map/answer/pallas_call | solution.py:548
  33.1 13.7 %all-to-all-start.1 = ((f32[256,1,128]{2,1,0:T(1,128)}), f32[256,1,128]{2,1,0:T(1,128)S(1)}, u32[]{:S(2)}, u32[]{:S(2)}) async-start(f32[256,1,128]{2,1,0:T(1,128)} %bitcast.4), calls=%async_computation.1 | async-start | bytes 262144 | tf_op jit(solution)/shard_map/all_to_all | solution.py:513
  46.8 0.0 copy-start.7
  46.9 1.3 %collective-permute-start = (f32[32,128]{1,0:T(8,128)S(1)}, f32[32,128]{1,0:T(8,128)S(1)}, u32[]{:S(2)}, u32[]{:S(2)}) collective-permute-start(f32[32,128]{1,0:T(8,128)S(1)} %get-tuple-element.29), channel_id=1, source_target_pairs={{0,1},{1,2},{2,3},{3,4},{4,5},{5,6},{6,7},{7,8},{8,9},{9,10},{10,1... | collective-permute-start | bytes 49160 | tf_op jit(solution)/shard_map/ppermute | solution.py:565
  48.2 2.6 %collective-permute-start.5 = (f32[32,128]{1,0:T(8,128)S(1)}, f32[32,128]{1,0:T(8,128)S(1)}, u32[]{:S(2)}, u32[]{:S(2)}) collective-permute-start(f32[32,128]{1,0:T(8,128)S(1)} %get-tuple-element.24), channel_id=1, source_target_pairs={{0,2},{1,3},{2,4},{3,5},{4,6},{5,7},{6,8},{7,9},{8,10},{9,11},{10,... | collective-permute-start | bytes 49160 | tf_op jit(solution)/shard_map/ppermute | solution.py:565
  50.7 3.8 %collective-permute-start.4 = (f32[32,128]{1,0:T(8,128)S(1)}, f32[32,128]{1,0:T(8,128)S(1)}, u32[]{:S(2)}, u32[]{:S(2)}) collective-permute-start(f32[32,128]{1,0:T(8,128)S(1)} %get-tuple-element.25), channel_id=1, source_target_pairs={{0,255},{1,0},{2,1},{3,2},{4,3},{5,4},{6,5},{7,6},{8,7},{9,8},{10,... | collective-permute-start | bytes 49160 | tf_op jit(solution)/shard_map/ppermute | solution.py:565
  54.5 2.8 %collective-permute-start.3 = (f32[32,128]{1,0:T(8,128)S(1)}, f32[32,128]{1,0:T(8,128)S(1)}, u32[]{:S(2)}, u32[]{:S(2)}) collective-permute-start(f32[32,128]{1,0:T(8,128)S(1)} %get-tuple-element.26), channel_id=1, source_target_pairs={{0,254},{1,255},{2,0},{3,1},{4,2},{5,3},{6,4},{7,5},{8,6},{9,7},{1... | collective-permute-start | bytes 49160 | tf_op jit(solution)/shard_map/ppermute | solution.py:565
  57.3 3.0 %collective-permute-start.1 = (f32[32,128]{1,0:T(8,128)S(1)}, f32[32,128]{1,0:T(8,128)S(1)}, u32[]{:S(2)}, u32[]{:S(2)}) collective-permute-start(f32[32,128]{1,0:T(8,128)S(1)} %get-tuple-element.28), channel_id=1, source_target_pairs={{0,32},{1,33},{2,34},{3,35},{4,36},{5,37},{6,38},{7,39},{8,40},{9,... | collective-permute-start | bytes 49160 | tf_op jit(solution)/shard_map/ppermute | solution.py:565
  60.3 3.6 %late_leaves.1.late_ref = f32[4,2,24,128]{3,2,1,0:T(8,128)S(1)} custom-call(s32[512]{0:T(512)S(1)} %copy-done.6, s32[1,3,128]{2,1,0:T(4,128)S(1)} %copy.18.leaf_pairs_ref, f32[3,512,128]{2,1,0:T(8,128)S(1)} %copy-done.1, f32[512,128]{1,0:T(8,128)S(1)} %copy-done.2), custom_call_target="tpu_custom_call" | custom-call | flops 20000000 | bytes 1500000 | tf_op jit(solution)/shard_map/late_leaves/pallas_call | solution.py:583
  63.9 0.0 copy-start.3
  63.9 2.4 %local_nodes.1.local_ref = f32[32,256]{1,0:T(8,128)S(1)} custom-call(s32[1,3,2048]{2,1,0:T(4,128)S(1)} %copy.17.pairs_ref, f32[32,256]{1,0:T(8,128)S(1)} %copy-done.5), custom_call_target="tpu_custom_call" | custom-call | flops 300000000 | bytes 300000 | tf_op jit(solution)/shard_map/local_nodes/pallas_call | solution.py:573
  66.3 0.0 collective-permute-done.5.cells4
  66.3 0.0 collective-permute-done.4.cells3
  66.3 0.0 collective-permute-done.3.cells2
  66.4 0.0 collective-permute-done.1.cells0
  66.4 4.5 %final.1 = (f32[35,256]{1,0:T(8,128)}, f32[3,512,128]{2,1,0:T(8,128)}) custom-call(s32[1,3,8,128]{3,2,1,0:T(8,128)S(1)} %copy-done.4, s32[6,8]{1,0:T(8,128)S(1)} %get-tuple-element.16.asked_ref, s32[512]{0:T(512)S(1)} %copy-done.6, f32[256,128]{1,0:T(8,128)S(1)} %copy-done.3, f32[256,128]{1,0:T(8,128)S(1)} %bitcast.21, ...), custom_call_target="tpu_custom_call" | custom-call | tf_op jit(solution)/shard_map/final/pallas_call | solution.py:593
  (20 shorter events, 0.1 us)
Async XLA Ops:
  0.6 17.1 %copy-start.2 = (f32[512,128]{1,0:T(8,128)S(1)}, f32[512,128]{1,0:T(8,128)}, u32[]{:S(2)}) copy-start(f32[512,128]{1,0:T(8,128)} %masses_ref.5) | copy-start | bytes 786436
  2.8 15.0 %copy-start.8 = (s32[1,3,128]{2,0,1:T(1,128)S(1)}, s32[1,3,128]{2,0,1:T(1,128)}, u32[]{:S(2)}) copy-start(s32[1,3,128]{2,0,1:T(1,128)} %param.15) | copy-start | bytes 4612
  2.8 26.5 %all-to-all-start = ((f32[256,1,128]{2,1,0:T(1,128)}), f32[256,1,128]{2,1,0:T(1,128)S(1)}, u32[]{:S(2)}, u32[]{:S(2)}) async-start(f32[256,1,128]{2,1,0:T(1,128)} %bitcast.20), calls=%async_computation | async-start | bytes 262144 | tf_op jit(solution)/shard_map/all_to_all | solution.py:513
  17.7 0.7 copy-start.6
  18.4 1.1 %copy-start = (f32[3,512,128]{2,1,0:T(8,128)S(1)}, f32[3,512,128]{2,1,0:T(8,128)}, u32[]{:S(2)}) copy-start(f32[3,512,128]{2,1,0:T(8,128)} %positions_ref.7) | copy-start | bytes 2359300
  19.6 9.7 %copy-start.1 = (f32[3,512,128]{2,1,0:T(8,128)S(1)}, f32[3,512,128]{2,1,0:T(8,128)}, u32[]{:S(2)}) copy-start(f32[3,512,128]{2,1,0:T(8,128)} %positions_ref.7) | copy-start | bytes 2359300
  19.6 9.7 %copy-start.4 = (s32[1,3,8,128]{3,2,1,0:T(8,128)S(1)}, s32[1,3,8,128]{3,2,1,0:T(8,128)}, u32[]{:S(2)}) copy-start(s32[1,3,8,128]{3,2,1,0:T(8,128)} %links_ref.3) | copy-start | bytes 36868
  19.6 9.7 %copy-start.5 = (f32[32,256]{1,0:T(8,128)S(1)}, f32[32,256]{1,0:T(8,128)}, u32[]{:S(2)}) copy-start(f32[32,256]{1,0:T(8,128)} %get-tuple-element.20.kept_ref) | copy-start | bytes 98308
  33.1 33.3 %all-to-all-start.1 = ((f32[256,1,128]{2,1,0:T(1,128)}), f32[256,1,128]{2,1,0:T(1,128)S(1)}, u32[]{:S(2)}, u32[]{:S(2)}) async-start(f32[256,1,128]{2,1,0:T(1,128)} %bitcast.4), calls=%async_computation.1 | async-start | bytes 262144 | tf_op jit(solution)/shard_map/all_to_all | solution.py:513
  46.8 1.3 %copy-start.7 = (s32[1,3,2048]{2,0,1:T(1,128)S(1)}, s32[1,3,2048]{2,0,1:T(1,128)}, u32[]{:S(2)}) copy-start(s32[1,3,2048]{2,0,1:T(1,128)} %param.14) | copy-start | bytes 73732
  46.9 10.5 %collective-permute-start = (f32[32,128]{1,0:T(8,128)S(1)}, f32[32,128]{1,0:T(8,128)S(1)}, u32[]{:S(2)}, u32[]{:S(2)}) collective-permute-start(f32[32,128]{1,0:T(8,128)S(1)} %get-tuple-element.29), channel_id=1, source_target_pairs={{0,1},{1,2},{2,3},{3,4},{4,5},{5,6},{6,7},{7,8},{8,9},{9,10},{10,1... | collective-permute-start | bytes 49160 | tf_op jit(solution)/shard_map/ppermute | solution.py:565
  48.2 18.2 %collective-permute-start.5 = (f32[32,128]{1,0:T(8,128)S(1)}, f32[32,128]{1,0:T(8,128)S(1)}, u32[]{:S(2)}, u32[]{:S(2)}) collective-permute-start(f32[32,128]{1,0:T(8,128)S(1)} %get-tuple-element.24), channel_id=1, source_target_pairs={{0,2},{1,3},{2,4},{3,5},{4,6},{5,7},{6,8},{7,9},{8,10},{9,11},{10,... | collective-permute-start | bytes 49160 | tf_op jit(solution)/shard_map/ppermute | solution.py:565
  50.7 15.6 %collective-permute-start.4 = (f32[32,128]{1,0:T(8,128)S(1)}, f32[32,128]{1,0:T(8,128)S(1)}, u32[]{:S(2)}, u32[]{:S(2)}) collective-permute-start(f32[32,128]{1,0:T(8,128)S(1)} %get-tuple-element.25), channel_id=1, source_target_pairs={{0,255},{1,0},{2,1},{3,2},{4,3},{5,4},{6,5},{7,6},{8,7},{9,8},{10,... | collective-permute-start | bytes 49160 | tf_op jit(solution)/shard_map/ppermute | solution.py:565
  54.5 11.8 %collective-permute-start.3 = (f32[32,128]{1,0:T(8,128)S(1)}, f32[32,128]{1,0:T(8,128)S(1)}, u32[]{:S(2)}, u32[]{:S(2)}) collective-permute-start(f32[32,128]{1,0:T(8,128)S(1)} %get-tuple-element.26), channel_id=1, source_target_pairs={{0,254},{1,255},{2,0},{3,1},{4,2},{5,3},{6,4},{7,5},{8,6},{9,7},{1... | collective-permute-start | bytes 49160 | tf_op jit(solution)/shard_map/ppermute | solution.py:565
  57.3 9.0 %collective-permute-start.2 = (f32[32,128]{1,0:T(8,128)S(1)}, f32[32,128]{1,0:T(8,128)S(1)}, u32[]{:S(2)}, u32[]{:S(2)}) collective-permute-start(f32[32,128]{1,0:T(8,128)S(1)} %get-tuple-element.27), channel_id=1, source_target_pairs={{0,224},{1,225},{2,226},{3,227},{4,228},{5,229},{6,230},{7,231},{8... | collective-permute-start | bytes 49160 | tf_op jit(solution)/shard_map/ppermute | solution.py:565
  57.3 9.0 %collective-permute-start.1 = (f32[32,128]{1,0:T(8,128)S(1)}, f32[32,128]{1,0:T(8,128)S(1)}, u32[]{:S(2)}, u32[]{:S(2)}) collective-permute-start(f32[32,128]{1,0:T(8,128)S(1)} %get-tuple-element.28), channel_id=1, source_target_pairs={{0,32},{1,33},{2,34},{3,35},{4,36},{5,37},{6,38},{7,39},{8,40},{9,... | collective-permute-start | bytes 49160 | tf_op jit(solution)/shard_map/ppermute | solution.py:565
  63.9 2.5 %copy-start.3 = (f32[256,128]{1,0:T(8,128)S(1)}, f32[256,128]{1,0:T(8,128)}, u32[]{:S(2)}) copy-start(f32[256,128]{1,0:T(8,128)} %get-tuple-element.13.sent_ref) | copy-start | bytes 393220

commit v3 on v2

--- a/solution.py
+++ b/solution.py
@@ -534,6 +534,17 @@
         name="pack",
     )(moments, node_links, leaf_links)
     got = exchange(sent)
+    local_exp = pl.pallas_call(
+        local_nodes_kernel,
+        out_shape=shape((32, 256), F32),
+        in_specs=[VMEM] * 2,
+        out_specs=VMEM,
+        scratch_shapes=[block] * 4,
+        compiler_params=PARAMS,
+        cost_estimate=pl.CostEstimate(flops=300_000_000, bytes_accessed=300_000, transcendentals=2048),
+        name="local_nodes",
+    )(node_local, kept)
+    leaf_early, local_exp = lax.optimization_barrier((leaf_local, local_exp))
     pull = pl.pallas_call(
         local_leaves_kernel,
         out_shape=shape(positions.shape, F32),
@@ -543,7 +554,7 @@
         compiler_params=PARAMS,
         cost_estimate=pl.CostEstimate(flops=80_000_000, bytes_accessed=3_000_000, transcendentals=2_100_000),
         name="local_leaves",
-    )(counts, leaf_local, positions, masses)
+    )(counts, leaf_early, positions, masses)
     got, pull = lax.optimization_barrier((got, pull))
     reply, cross, asked, cells = pl.pallas_call(
         answer_kernel,
@@ -569,17 +580,7 @@
         )
         for number, shift in enumerate(SHIFTS)
     ]
-    kept_late, leaf_pairs_late, moved[5] = lax.optimization_barrier((kept, leaf_local, moved[5]))
-    local_exp = pl.pallas_call(
-        local_nodes_kernel,
-        out_shape=shape((32, 256), F32),
-        in_specs=[VMEM] * 2,
-        out_specs=VMEM,
-        scratch_shapes=[block] * 4,
-        compiler_params=PARAMS,
-        cost_estimate=pl.CostEstimate(flops=300_000_000, bytes_accessed=300_000, transcendentals=2048),
-        name="local_nodes",
-    )(node_local, kept_late)
+    leaf_pairs_late, moved[5] = lax.optimization_barrier((leaf_local, moved[5]))
     late = pl.pallas_call(
         late_leaves_kernel,
         out_shape=shape((CHAINS, 2, 24, 128), F32),

time: 71.2 us -> 71 us (level)
    unnamed x20 -> x18, local copies, waits for them, and re-layouts: 1.84 us -> 2.2 us
  transfers between devices with their start and end apart: 8 -> 8, of which waited for: 0 -> 0; matrix products, arithmetic and copies ran while one was open for 0% -> 1% of each run, Pallas kernels for 22% -> 22%
where the time goes in v3:
time: 71 us; the launch traced here: 70.7 us
  starting transfers between devices  41.5 us (58%)
  Pallas kernels  26.1 us (37%)
  local copies, waits for them, and re-layouts  2.22 us (3%)
  between operations  0.83 us (1%)
    all_to_all x2, starting transfers between devices, exchange(): lax.all_to_all(sent.reshape(DOMAINS, 1, 128), ('dx', 'dy'), split_axis=0,...  28.7 us
    ppermute x6, starting transfers between devices, on_device(): lax.ppermute(cells[number], ('dx', 'dy'), [(device, (device + shift) % DO...  12.8 us
    pallas_call x1, Pallas kernels, on_device(): pl.pallas_call(local_leaves_kernel, out_shape=shape(positions.shape, F32)...  9.67 us
    pallas_call x1, Pallas kernels, on_device(): pl.pallas_call(final_kernel, out_shape=(shape(moments.shape, F32), shape(...  4.53 us
    pallas_call x1, Pallas kernels, on_device(): pl.pallas_call(answer_kernel, out_shape=(shape((256, 128), F32), shape((3...  3.83 us
    pallas_call x1, Pallas kernels, on_device(): pl.pallas_call(late_leaves_kernel, out_shape=shape((CHAINS, 2, 24, 128),...  3.55 us
    pallas_call x1, Pallas kernels, on_device(): pl.pallas_call(local_nodes_kernel, out_shape=shape((32, 256), F32), in_sp...  2.41 us
    unnamed x18, local copies, waits for them, and re-layouts  2.2 us
  transfers between devices with their start and end apart: 8, of which 0 were waited for; matrix products, arithmetic and copies ran while one was open for 1% of the time, Pallas kernels for 22%

profile of v3, /device:TPU:7, one launch (start us, length us, event | category | flops | bytes accessed | tf_op | source)
XLA Modules:
  0.0 70.7 jit_solution(15258037113698657533)
XLA Ops:
  0.6 2.1 %pack.1 = (f32[32,256]{1,0:T(8,128)}, f32[256,128]{1,0:T(8,128)}) custom-call(f32[35,256]{1,0:T(8,128)} %moments_hbm.1, s32[1,3,8,128]{3,2,1,0:T(8,128)} %nodes_hbm.1, s32[1,3,8,128]{3,2,1,0:T(8,128)} %links_ref.3), custom_call_target="tpu_custom_call" | custom-call | tf_op jit(solution)/shard_map/pack/pallas_call | solution.py:522
  2.8 15.0 %all-to-all-start = ((f32[256,1,128]{2,1,0:T(1,128)}), f32[256,1,128]{2,1,0:T(1,128)S(1)}, u32[]{:S(2)}, u32[]{:S(2)}) async-start(f32[256,1,128]{2,1,0:T(1,128)} %bitcast.20), calls=%async_computation | async-start | bytes 262144 | tf_op jit(solution)/shard_map/all_to_all | solution.py:513
  17.7 0.8 %copy.15.pairs_ref = s32[1,3,2048]{2,1,0:T(4,128)S(1)} copy(s32[1,3,2048]{2,0,1:T(1,128)} %param.14) | data formatting | bytes 49152 | tf_op args[6]
  18.5 0.0 copy-start.4
  18.5 0.7 %copy-done.4 = f32[32,256]{1,0:T(8,128)S(1)} copy-done((f32[32,256]{1,0:T(8,128)S(1)}, f32[32,256]{1,0:T(8,128)}, u32[]{:S(2)}) %copy-start.4) | copy-done | bytes 32792
  19.3 2.4 %local_nodes.1.local_ref = f32[32,256]{1,0:T(8,128)S(1)} custom-call(s32[1,3,2048]{2,1,0:T(4,128)S(1)} %copy.15.pairs_ref, f32[32,256]{1,0:T(8,128)S(1)} %copy-done.4), custom_call_target="tpu_custom_call" | custom-call | flops 300000000 | bytes 300000 | tf_op jit(solution)/shard_map/local_nodes/pallas_call | solution.py:537
  21.7 0.0 copy-done.7
  21.7 0.0 copy-start.6
  21.8 0.6 copy-done.6
  22.4 9.7 %local_leaves.1.pull_ref = f32[3,512,128]{2,1,0:T(8,128)S(1)} custom-call(s32[512]{0:T(512)S(1)} %copy-done.6, s32[1,3,128]{2,1,0:T(4,128)S(1)} %copy.16.leaf_pairs_ref, f32[3,512,128]{2,1,0:T(8,128)S(1)} %copy-done, f32[512,128]{1,0:T(8,128)S(1)} %copy-done.1), custom_call_target="tpu_custom_call" | custom-call | flops 80000000 | bytes 3000000 | tf_op jit(solution)/shard_map/local_leaves/pallas_call | solution.py:548
  32.1 0.0 all-to-all-done
  32.1 3.8 %answer.1 = (f32[256,128]{1,0:T(8,128)}, f32[32,256]{1,0:T(8,128)S(1)}, s32[6,8]{1,0:T(8,128)S(1)}, f32[6,32,128]{2,1,0:T(8,128)S(1)}) custom-call(s32[1,3,8,128]{3,2,1,0:T(8,128)S(1)} %copy-done.3, s32[512]{0:T(512)S(1)} %copy-done.6, f32[256,128]{1,0:T(8,128)S(1)} %bitcast.22, f32[32,256]{1,0:T(8,128)S(1)} %copy-done.5, f32[3,512,128]{2,1,0:T(8,128)S(1)} %copy-done, ...), custom_call_target="tpu_custom_call" | custom-call | tf_op jit(solution)/shard_map/answer/pallas_call | solution.py:559
  35.9 13.7 %all-to-all-start.1 = ((f32[256,1,128]{2,1,0:T(1,128)}), f32[256,1,128]{2,1,0:T(1,128)S(1)}, u32[]{:S(2)}, u32[]{:S(2)}) async-start(f32[256,1,128]{2,1,0:T(1,128)} %bitcast.4), calls=%async_computation.1 | async-start | bytes 262144 | tf_op jit(solution)/shard_map/all_to_all | solution.py:513
  49.7 1.3 %collective-permute-start.5 = (f32[32,128]{1,0:T(8,128)S(1)}, f32[32,128]{1,0:T(8,128)S(1)}, u32[]{:S(2)}, u32[]{:S(2)}) collective-permute-start(f32[32,128]{1,0:T(8,128)S(1)} %get-tuple-element.26), channel_id=1, source_target_pairs={{0,1},{1,2},{2,3},{3,4},{4,5},{5,6},{6,7},{7,8},{8,9},{9,10},{10,1... | collective-permute-start | bytes 49160 | tf_op jit(solution)/shard_map/ppermute | solution.py:576
  51.0 2.5 %collective-permute-start.4 = (f32[32,128]{1,0:T(8,128)S(1)}, f32[32,128]{1,0:T(8,128)S(1)}, u32[]{:S(2)}, u32[]{:S(2)}) collective-permute-start(f32[32,128]{1,0:T(8,128)S(1)} %get-tuple-element.27), channel_id=1, source_target_pairs={{0,2},{1,3},{2,4},{3,5},{4,6},{5,7},{6,8},{7,9},{8,10},{9,11},{10,... | collective-permute-start | bytes 49160 | tf_op jit(solution)/shard_map/ppermute | solution.py:576
  53.4 3.5 %collective-permute-start.3 = (f32[32,128]{1,0:T(8,128)S(1)}, f32[32,128]{1,0:T(8,128)S(1)}, u32[]{:S(2)}, u32[]{:S(2)}) collective-permute-start(f32[32,128]{1,0:T(8,128)S(1)} %get-tuple-element.28), channel_id=1, source_target_pairs={{0,255},{1,0},{2,1},{3,2},{4,3},{5,4},{6,5},{7,6},{8,7},{9,8},{10,... | collective-permute-start | bytes 49160 | tf_op jit(solution)/shard_map/ppermute | solution.py:576
  56.9 2.6 %collective-permute-start.2 = (f32[32,128]{1,0:T(8,128)S(1)}, f32[32,128]{1,0:T(8,128)S(1)}, u32[]{:S(2)}, u32[]{:S(2)}) collective-permute-start(f32[32,128]{1,0:T(8,128)S(1)} %get-tuple-element.29), channel_id=1, source_target_pairs={{0,254},{1,255},{2,0},{3,1},{4,2},{5,3},{6,4},{7,5},{8,6},{9,7},{1... | collective-permute-start | bytes 49160 | tf_op jit(solution)/shard_map/ppermute | solution.py:576
  59.5 0.0 collective-permute-start.1
  59.5 0.0 collective-permute-done.5.cells5
  59.5 3.0 %collective-permute-start = (f32[32,128]{1,0:T(8,128)S(1)}, f32[32,128]{1,0:T(8,128)S(1)}, u32[]{:S(2)}, u32[]{:S(2)}) collective-permute-start(f32[32,128]{1,0:T(8,128)S(1)} %get-tuple-element.31), channel_id=1, source_target_pairs={{0,32},{1,33},{2,34},{3,35},{4,36},{5,37},{6,38},{7,39},{8,40},{9,... | collective-permute-start | bytes 49160 | tf_op jit(solution)/shard_map/ppermute | solution.py:576
  62.5 3.5 %late_leaves.1.late_ref = f32[4,2,24,128]{3,2,1,0:T(8,128)S(1)} custom-call(s32[512]{0:T(512)S(1)} %copy-done.6, s32[1,3,128]{2,1,0:T(4,128)S(1)} %copy.18.leaf_pairs_ref, f32[3,512,128]{2,1,0:T(8,128)S(1)} %copy-done, f32[512,128]{1,0:T(8,128)S(1)} %copy-done.1), custom_call_target="tpu_custom_call" | custom-call | flops 20000000 | bytes 1500000 | tf_op jit(solution)/shard_map/late_leaves/pallas_call | solution.py:584
  66.1 0.0 collective-permute-done.4.cells4
  66.1 0.0 collective-permute-done.3.cells3
  66.1 4.5 %final.1 = (f32[35,256]{1,0:T(8,128)}, f32[3,512,128]{2,1,0:T(8,128)}) custom-call(s32[1,3,8,128]{3,2,1,0:T(8,128)S(1)} %copy-done.3, s32[6,8]{1,0:T(8,128)S(1)} %get-tuple-element.18.asked_ref, s32[512]{0:T(512)S(1)} %copy-done.6, f32[256,128]{1,0:T(8,128)S(1)} %copy-done.2, f32[256,128]{1,0:T(8,128)S(1)} %bitcast.21, ...), custom_call_target="tpu_custom_call" | custom-call | tf_op jit(solution)/shard_map/final/pallas_call | solution.py:594
  (19 shorter events, 0.0 us)
Async XLA Ops:
  0.6 21.1 %copy-start = (f32[3,512,128]{2,1,0:T(8,128)S(1)}, f32[3,512,128]{2,1,0:T(8,128)}, u32[]{:S(2)}) copy-start(f32[3,512,128]{2,1,0:T(8,128)} %positions_ref.7) | copy-start | bytes 2359300
  2.8 29.3 %all-to-all-start = ((f32[256,1,128]{2,1,0:T(1,128)}), f32[256,1,128]{2,1,0:T(1,128)S(1)}, u32[]{:S(2)}, u32[]{:S(2)}) async-start(f32[256,1,128]{2,1,0:T(1,128)} %bitcast.20), calls=%async_computation | async-start | bytes 262144 | tf_op jit(solution)/shard_map/all_to_all | solution.py:513
  18.5 0.8 %copy-start.4 = (f32[32,256]{1,0:T(8,128)S(1)}, f32[32,256]{1,0:T(8,128)}, u32[]{:S(2)}) copy-start(f32[32,256]{1,0:T(8,128)} %get-tuple-element.15.kept_ref) | copy-start | bytes 98308
  19.3 2.4 %copy-start.7 = (s32[1,3,128]{2,0,1:T(1,128)S(1)}, s32[1,3,128]{2,0,1:T(1,128)}, u32[]{:S(2)}) copy-start(s32[1,3,128]{2,0,1:T(1,128)} %param.15) | copy-start | bytes 4612
  19.3 2.5 %copy-start.1 = (f32[512,128]{1,0:T(8,128)S(1)}, f32[512,128]{1,0:T(8,128)}, u32[]{:S(2)}) copy-start(f32[512,128]{1,0:T(8,128)} %masses_ref.5) | copy-start | bytes 786436
  21.7 0.7 copy-start.6
  22.4 9.7 %copy-start.3 = (s32[1,3,8,128]{3,2,1,0:T(8,128)S(1)}, s32[1,3,8,128]{3,2,1,0:T(8,128)}, u32[]{:S(2)}) copy-start(s32[1,3,8,128]{3,2,1,0:T(8,128)} %links_ref.3) | copy-start | bytes 36868
  22.4 9.7 %copy-start.5 = (f32[32,256]{1,0:T(8,128)S(1)}, f32[32,256]{1,0:T(8,128)}, u32[]{:S(2)}) copy-start(f32[32,256]{1,0:T(8,128)} %get-tuple-element.15.kept_ref) | copy-start | bytes 98308
  35.9 30.2 %all-to-all-start.1 = ((f32[256,1,128]{2,1,0:T(1,128)}), f32[256,1,128]{2,1,0:T(1,128)S(1)}, u32[]{:S(2)}, u32[]{:S(2)}) async-start(f32[256,1,128]{2,1,0:T(1,128)} %bitcast.4), calls=%async_computation.1 | async-start | bytes 262144 | tf_op jit(solution)/shard_map/all_to_all | solution.py:513
  49.7 9.8 %collective-permute-start.5 = (f32[32,128]{1,0:T(8,128)S(1)}, f32[32,128]{1,0:T(8,128)S(1)}, u32[]{:S(2)}, u32[]{:S(2)}) collective-permute-start(f32[32,128]{1,0:T(8,128)S(1)} %get-tuple-element.26), channel_id=1, source_target_pairs={{0,1},{1,2},{2,3},{3,4},{4,5},{5,6},{6,7},{7,8},{8,9},{9,10},{10,1... | collective-permute-start | bytes 49160 | tf_op jit(solution)/shard_map/ppermute | solution.py:576
  51.0 15.1 %collective-permute-start.4 = (f32[32,128]{1,0:T(8,128)S(1)}, f32[32,128]{1,0:T(8,128)S(1)}, u32[]{:S(2)}, u32[]{:S(2)}) collective-permute-start(f32[32,128]{1,0:T(8,128)S(1)} %get-tuple-element.27), channel_id=1, source_target_pairs={{0,2},{1,3},{2,4},{3,5},{4,6},{5,7},{6,8},{7,9},{8,10},{9,11},{10,... | collective-permute-start | bytes 49160 | tf_op jit(solution)/shard_map/ppermute | solution.py:576
  53.4 12.6 %collective-permute-start.3 = (f32[32,128]{1,0:T(8,128)S(1)}, f32[32,128]{1,0:T(8,128)S(1)}, u32[]{:S(2)}, u32[]{:S(2)}) collective-permute-start(f32[32,128]{1,0:T(8,128)S(1)} %get-tuple-element.28), channel_id=1, source_target_pairs={{0,255},{1,0},{2,1},{3,2},{4,3},{5,4},{6,5},{7,6},{8,7},{9,8},{10,... | collective-permute-start | bytes 49160 | tf_op jit(solution)/shard_map/ppermute | solution.py:576
  56.9 9.1 %collective-permute-start.2 = (f32[32,128]{1,0:T(8,128)S(1)}, f32[32,128]{1,0:T(8,128)S(1)}, u32[]{:S(2)}, u32[]{:S(2)}) collective-permute-start(f32[32,128]{1,0:T(8,128)S(1)} %get-tuple-element.29), channel_id=1, source_target_pairs={{0,254},{1,255},{2,0},{3,1},{4,2},{5,3},{6,4},{7,5},{8,6},{9,7},{1... | collective-permute-start | bytes 49160 | tf_op jit(solution)/shard_map/ppermute | solution.py:576
  59.5 6.6 %collective-permute-start.1 = (f32[32,128]{1,0:T(8,128)S(1)}, f32[32,128]{1,0:T(8,128)S(1)}, u32[]{:S(2)}, u32[]{:S(2)}) collective-permute-start(f32[32,128]{1,0:T(8,128)S(1)} %get-tuple-element.30), channel_id=1, source_target_pairs={{0,224},{1,225},{2,226},{3,227},{4,228},{5,229},{6,230},{7,231},{8... | collective-permute-start | bytes 49160 | tf_op jit(solution)/shard_map/ppermute | solution.py:576
  59.5 6.6 %collective-permute-start = (f32[32,128]{1,0:T(8,128)S(1)}, f32[32,128]{1,0:T(8,128)S(1)}, u32[]{:S(2)}, u32[]{:S(2)}) collective-permute-start(f32[32,128]{1,0:T(8,128)S(1)} %get-tuple-element.31), channel_id=1, source_target_pairs={{0,32},{1,33},{2,34},{3,35},{4,36},{5,37},{6,38},{7,39},{8,40},{9,... | collective-permute-start | bytes 49160 | tf_op jit(solution)/shard_map/ppermute | solution.py:576
  62.5 3.6 %copy-start.2 = (f32[256,128]{1,0:T(8,128)S(1)}, f32[256,128]{1,0:T(8,128)}, u32[]{:S(2)}) copy-start(f32[256,128]{1,0:T(8,128)} %get-tuple-element.14.sent_ref) | copy-start | bytes 393220
